TPU v7x, 128 devices: a whole 4x4x4 slice. The times are simulated.
128 devices in a mesh: band: 2 (over z_lo), prow: 4 (over x), pcol: 16 (over y, z_hi, core).
Axes of the slice: x: 4, y: 4, z: 4 (z_hi: 2, z_lo: 2; z = z_hi * 2 + z_lo), core: 2. Of those that a mesh axis runs over, the one named last changes fastest.
Arguments:
- orbitals: float32 [4, 192, 192, 192], P('band', 'prow', 'pcol'), may hold values from -6 to 6
- kernel: float32 [192, 192, 192], P('prow', 'pcol'), as said below
- plan: int32 [4], replicated, may hold values from 0 to 3, each once
- occupation: int32 [4], replicated, may hold values 0 or 1
Outputs:
- exchange_orbitals: float32 [4, 192, 192, 192], P('band', 'prow', 'pcol')
Inputs may be any that keep to these rules, and one draw needn't show every extreme that they name: `plan`: a permutation of the blocks; entry e names block e % (2) of band group e // 2; this window treats the blocks of its first 2 entries. kernel at (ky, kz, kx) equals kernel at (-ky, -kz, -kx), indices taken modulo 192.
All inputs are finite; a program needn't handle non-finite values.
Results may differ from a plain program's by a relative error of at most 0.00014.
Values sent between devices are 32-bit elements; how exact they have to be, the bound alone decides.
A program may use at most 128 MiB of HBM per device.

v0:
```python
import math

import jax
import jax.numpy as jnp
from jax import lax
from jax.sharding import PartitionSpec as P

IBLK = 1
ROUNDS = 2


def from_root(block, axis, source):
    block = jnp.where(lax.axis_index(axis) == source, block, jnp.zeros_like(block))
    return lax.psum(block, axis)


def tables(length):
    indices = jnp.arange(length, dtype=jnp.int32)
    product = indices[:, None] * indices[None, :] % length
    angles = product.astype(jnp.float32) * (2.0 * math.pi / length)
    return (jnp.cos(angles), jnp.sin(angles))


def contract(form, left, right):
    return jnp.einsum(
        form, left, right, precision=lax.Precision.HIGHEST, preferred_element_type=jnp.float32
    )


def fetch_block(orbitals, plan, occupation, round_id):
    per_owner = orbitals.shape[0] // IBLK
    block_id = plan[round_id]
    owner_id = block_id // per_owner
    offset = block_id % per_owner * IBLK
    own_block = lax.dynamic_slice_in_dim(orbitals, offset, IBLK, 0)
    block = from_root(own_block, "band", owner_id)
    weights = lax.dynamic_slice_in_dim(occupation, owner_id * orbitals.shape[0] + offset, IBLK, 0)
    return (block, weights.astype(jnp.float32) * -0.25)


def potentials(density, kernel):
    y_local, amount, x_local, length = density.shape
    cosine, sine_table = tables(length)
    flat = density.reshape((-1, length))
    spec_real = contract("zk,rz->kr", cosine, flat)
    spec_imag = -contract("zk,rz->kr", sine_table, flat)
    spec_real = spec_real.reshape((length, y_local, amount * x_local))
    spec_imag = spec_imag.reshape((length, y_local, amount * x_local))
    spec_real, spec_imag = (
        lax.all_to_all(spec_real, "pcol", split_axis=0, concat_axis=1, tiled=True),
        lax.all_to_all(spec_imag, "pcol", split_axis=0, concat_axis=1, tiled=True),
    )
    kz_local = spec_real.shape[0]
    mid_real = contract("yl,kyr->lkr", cosine, spec_real) + contract(
        "yl,kyr->lkr", sine_table, spec_imag
    )
    mid_imag = contract("yl,kyr->lkr", cosine, spec_imag) - contract(
        "yl,kyr->lkr", sine_table, spec_real
    )
    mid_real = mid_real.reshape((length, kz_local, amount, x_local))
    mid_imag = mid_imag.reshape((length, kz_local, amount, x_local))
    mid_real, mid_imag = (
        lax.all_to_all(mid_real, "prow", split_axis=0, concat_axis=3, tiled=True),
        lax.all_to_all(mid_imag, "prow", split_axis=0, concat_axis=3, tiled=True),
    )
    ky_local = mid_real.shape[0]
    mid_real = mid_real.reshape((-1, length))
    mid_imag = mid_imag.reshape((-1, length))
    expanded = jnp.broadcast_to(
        jnp.transpose(kernel, (2, 0, 1))[..., None], (length, ky_local, kz_local, amount)
    )
    expanded = expanded.reshape((length, -1)) * (1.0 / length**3)
    freq_real = (
        contract("xm,rx->mr", cosine, mid_real) + contract("xm,rx->mr", sine_table, mid_imag)
    ) * expanded
    freq_imag = (
        contract("xm,rx->mr", cosine, mid_imag) - contract("xm,rx->mr", sine_table, mid_real)
    ) * expanded
    back_real = contract("mr,mx->rx", freq_real, cosine) - contract(
        "mr,mx->rx", freq_imag, sine_table
    )
    back_imag = contract("mr,mx->rx", freq_imag, cosine) + contract(
        "mr,mx->rx", freq_real, sine_table
    )
    back_real = back_real.reshape((ky_local, kz_local, amount, length))
    back_imag = back_imag.reshape((ky_local, kz_local, amount, length))
    back_real, back_imag = (
        lax.all_to_all(back_real, "prow", split_axis=3, concat_axis=0, tiled=True),
        lax.all_to_all(back_imag, "prow", split_axis=3, concat_axis=0, tiled=True),
    )
    back_real = back_real.reshape((length, -1))
    back_imag = back_imag.reshape((length, -1))
    near_real = contract("ly,lr->yr", cosine, back_real) - contract(
        "ly,lr->yr", sine_table, back_imag
    )
    near_imag = contract("ly,lr->yr", cosine, back_imag) + contract(
        "ly,lr->yr", sine_table, back_real
    )
    near_real = near_real.reshape((length, kz_local, amount * x_local))
    near_imag = near_imag.reshape((length, kz_local, amount * x_local))
    near_real, near_imag = (
        lax.all_to_all(near_real, "pcol", split_axis=0, concat_axis=1, tiled=True),
        lax.all_to_all(near_imag, "pcol", split_axis=0, concat_axis=1, tiled=True),
    )
    field = contract("ykr,kz->yrz", near_real, cosine) - contract(
        "ykr,kz->yrz", near_imag, sine_table
    )
    return field.reshape((y_local, amount, x_local, length))


def on_device(orbitals, kernel, plan, occupation):
    bands_here = orbitals.shape[0]
    laid = jnp.transpose(orbitals, (2, 0, 1, 3))
    summed = jnp.zeros(laid.shape, jnp.float32)
    for round_id in range(ROUNDS):
        block, weights = fetch_block(orbitals, plan, occupation, round_id)
        members = block.shape[0]
        turned = jnp.transpose(block, (2, 0, 1, 3))
        y_local, _, x_local, length = laid.shape
        density = (turned[:, :, None] * laid[:, None]).reshape(
            (y_local, members * bands_here, x_local, length)
        )
        fields = potentials(density, kernel).reshape(
            (y_local, members, bands_here, x_local, length)
        )
        summed = summed + jnp.sum(
            weights[None, :, None, None, None] * fields * turned[:, :, None], axis=1
        )
    return jnp.transpose(summed, (1, 2, 0, 3))


def solution(mesh):
    return jax.shard_map(
        on_device,
        mesh=mesh,
        in_specs=(P("band", "prow", "pcol", None), P("prow", "pcol", None), P(), P()),
        out_specs=P("band", "prow", "pcol", None),
        check_vma=False,
    )
```

profile of v0, /device:TPU:1, one launch (start us, length us, event | category | flops | bytes accessed | tf_op | source)
XLA Modules:
  0.0 630.5 jit_solution(11257588911481026405)
XLA Ops:
  15.5 53.2 %all-reduce.3.cloned.1.call-done = (f32[12,48,192]{2,1,0:T(8,128)}, f32[12,48,192]{2,1,0:T(8,128)}) async-done(((f32[12,48,192]{2,1,0:T(8,128)}, f32[12,48,192]{2,1,0:T(8,128)}), (f32[12,48,192]{2,1,0:T(8,128)}, f32[12,48,192]{2,1,0:T(8,128)})) %all-reduce.3.cloned.1.call-update) | async-done | bytes 884752 | tf_op jit(solution)/shard_map/psum | solution.py:14
  78.0 7.3 %all-to-all-start.1 = ((f32[192,12,96]{2,1,0:T(8,128)}), f32[192,12,96]{2,1,0:T(8,128)}, u32[]{:S(2)}, u32[]{:S(2)}) async-start(f32[192,12,96]{2,1,0:T(8,128)} %copy.196), calls=%async_computation.1 | async-start | bytes 3145728 | tf_op jit(solution)/shard_map/all_to_all | solution.py:51
  90.3 17.9 %all-to-all-done.1 = f32[192,12,96]{2,1,0:T(8,128)} async-done(((f32[192,12,96]{2,1,0:T(8,128)}), f32[192,12,96]{2,1,0:T(8,128)}, u32[]{:S(2)}, u32[]{:S(2)}) %all-to-all-start.1) | async-done | bytes 884768 | tf_op jit(solution)/shard_map/all_to_all | solution.py:51
  108.2 5.6 all-to-all-start
  119.0 17.7 %all-to-all-done = f32[192,12,96]{2,1,0:T(8,128)} async-done(((f32[192,12,96]{2,1,0:T(8,128)}), f32[192,12,96]{2,1,0:T(8,128)}, u32[]{:S(2)}, u32[]{:S(2)}) %all-to-all-start) | async-done | bytes 884768 | tf_op jit(solution)/shard_map/all_to_all | solution.py:50
  164.7 5.3 all-to-all-start.8
  179.1 5.9 reshape.169
  187.9 5.1 all-to-all-done.8
  234.5 5.9 reshape.161
  246.4 5.3 reshape.159
  252.3 5.0 reduce.5
  279.8 5.3 reshape.168
  358.0 5.9 reshape.171
  368.0 5.3 reshape.160
  449.2 5.0 reduce.6
  462.4 5.0 reshape.123
  475.5 9.0 %all-to-all-start.7 = ((f32[192,12,96]{2,1,0:T(8,128)}), f32[192,12,96]{2,1,0:T(8,128)}, u32[]{:S(2)}, u32[]{:S(2)}) async-start(f32[192,12,96]{2,1,0:T(8,128)} %copy.223), calls=%async_computation.7 | async-start | bytes 3145728 | tf_op jit(solution)/shard_map/all_to_all | solution.py:103
  492.4 15.1 %all-to-all-done.7 = f32[192,12,96]{2,1,0:T(8,128)} async-done(((f32[192,12,96]{2,1,0:T(8,128)}), f32[192,12,96]{2,1,0:T(8,128)}, u32[]{:S(2)}, u32[]{:S(2)}) %all-to-all-start.7) | async-done | bytes 884768 | tf_op jit(solution)/shard_map/all_to_all | solution.py:103
  507.4 5.3 all-to-all-start.6
  528.7 5.0 reduce.2
  554.9 7.3 %all-to-all-start.15 = ((f32[192,12,96]{2,1,0:T(8,128)}), f32[192,12,96]{2,1,0:T(8,128)}, u32[]{:S(2)}, u32[]{:S(2)}) async-start(f32[192,12,96]{2,1,0:T(8,128)} %copy.259), calls=%async_computation.15 | async-start | bytes 3145728 | tf_op jit(solution)/shard_map/all_to_all | solution.py:103
  570.2 15.0 %all-to-all-done.15 = f32[192,12,96]{2,1,0:T(8,128)} async-done(((f32[192,12,96]{2,1,0:T(8,128)}), f32[192,12,96]{2,1,0:T(8,128)}, u32[]{:S(2)}, u32[]{:S(2)}) %all-to-all-start.15) | async-done | bytes 884768 | tf_op jit(solution)/shard_map/all_to_all | solution.py:103
  600.1 5.3 fusion.14
  605.3 7.5 %all-to-all-done.14 = f32[192,12,96]{2,1,0:T(8,128)S(1)} async-done(((f32[192,12,96]{2,1,0:T(8,128)}), f32[192,12,96]{2,1,0:T(8,128)S(1)}, u32[]{:S(2)}, u32[]{:S(2)}) %all-to-all-start.14) | async-done | bytes 884768 | tf_op jit(solution)/shard_map/all_to_all | solution.py:102
  (197 shorter events, 379.7 us)
Async XLA Ops:
  6.5 62.1 %all-reduce.3.cloned.1.call-start = ((), (), s32[]{:S(2)}) async-start(), calls=%async_computation.16 | async-start | bytes 2359296 | tf_op jit(solution)/shard_map/psum | solution.py:14
  78.0 30.2 %all-to-all-start.1 = ((f32[192,12,96]{2,1,0:T(8,128)}), f32[192,12,96]{2,1,0:T(8,128)}, u32[]{:S(2)}, u32[]{:S(2)}) async-start(f32[192,12,96]{2,1,0:T(8,128)} %copy.196), calls=%async_computation.1 | async-start | bytes 3145728 | tf_op jit(solution)/shard_map/all_to_all | solution.py:51
  108.2 28.5 %all-to-all-start = ((f32[192,12,96]{2,1,0:T(8,128)}), f32[192,12,96]{2,1,0:T(8,128)}, u32[]{:S(2)}, u32[]{:S(2)}) async-start(f32[192,12,96]{2,1,0:T(8,128)} %copy.191), calls=%async_computation | async-start | bytes 3145728 | tf_op jit(solution)/shard_map/all_to_all | solution.py:50
  119.0 22.7 %copy-start.18 = (f32[48,12,192]{2,0,1:T(8,128)S(1)}, f32[48,12,192]{2,0,1:T(8,128)}, u32[]{:S(2)}) copy-start(f32[48,12,192]{2,0,1:T(8,128)} %param.5) | copy-start | bytes 1327108
  136.7 28.0 %all-to-all-start.9 = ((f32[192,12,96]{2,1,0:T(8,128)}), f32[192,12,96]{2,1,0:T(8,128)}, u32[]{:S(2)}, u32[]{:S(2)}) async-start(f32[192,12,96]{2,1,0:T(8,128)} %copy.233), calls=%async_computation.9 | async-start | bytes 3145728 | tf_op jit(solution)/shard_map/all_to_all | solution.py:51
  164.7 28.2 %all-to-all-start.8 = ((f32[192,12,96]{2,1,0:T(8,128)}), f32[192,12,96]{2,1,0:T(8,128)}, u32[]{:S(2)}, u32[]{:S(2)}) async-start(f32[192,12,96]{2,1,0:T(8,128)} %copy.228), calls=%async_computation.8 | async-start | bytes 3145728 | tf_op jit(solution)/shard_map/all_to_all | solution.py:50
  192.9 32.4 %all-to-all-start.3 = ((f32[4,1,55296]{2,1,0:T(1,128)}), f32[4,1,55296]{2,1,0:T(1,128)}, u32[]{:S(2)}, u32[]{:S(2)}) async-start(f32[4,1,55296]{2,1,0:T(1,128)} %reshape.169), calls=%async_computation.3 | async-start | bytes 1769472 | tf_op jit(solution)/shard_map/all_to_all | solution.py:64
  225.4 45.9 %all-to-all-start.2 = ((f32[4,1,55296]{2,1,0:T(1,128)}), f32[4,1,55296]{2,1,0:T(1,128)}, u32[]{:S(2)}, u32[]{:S(2)}) async-start(f32[4,1,55296]{2,1,0:T(1,128)} %reshape.167), calls=%async_computation.2 | async-start | bytes 1769472 | tf_op jit(solution)/shard_map/all_to_all | solution.py:63
  271.3 33.2 %all-to-all-start.11 = ((f32[4,1,55296]{2,1,0:T(1,128)}), f32[4,1,55296]{2,1,0:T(1,128)}, u32[]{:S(2)}, u32[]{:S(2)}) async-start(f32[4,1,55296]{2,1,0:T(1,128)} %reshape.161), calls=%async_computation.11 | async-start | bytes 1769472 | tf_op jit(solution)/shard_map/all_to_all | solution.py:64
  296.3 5.4 copy-start.1
  304.5 7.6 %copy-start.3 = (f32[192,1152]{1,0:T(8,128)}, f32[192,1152]{1,0:T(8,128)S(1)}, u32[]{:S(2)}) copy-start(f32[192,1152]{1,0:T(8,128)S(1)} %fusion) | copy-start | bytes 2654212
  304.5 4.9 copy-start.13
  304.5 38.9 %all-to-all-start.10 = ((f32[4,1,55296]{2,1,0:T(1,128)}), f32[4,1,55296]{2,1,0:T(1,128)}, u32[]{:S(2)}, u32[]{:S(2)}) async-start(f32[4,1,55296]{2,1,0:T(1,128)} %reshape.159), calls=%async_computation.10 | async-start | bytes 1769472 | tf_op jit(solution)/shard_map/all_to_all | solution.py:63
  343.4 44.5 %all-to-all-start.5 = ((f32[4,1,55296]{2,1,0:T(1,128)}), f32[4,1,55296]{2,1,0:T(1,128)}, u32[]{:S(2)}, u32[]{:S(2)}) async-start(f32[4,1,55296]{2,1,0:T(1,128)} %reshape.173), calls=%async_computation.5 | async-start | bytes 1769472 | tf_op jit(solution)/shard_map/all_to_all | solution.py:89
  387.9 4.8 copy-start
  387.9 23.0 %all-to-all-start.4 = ((f32[4,1,55296]{2,1,0:T(1,128)}), f32[4,1,55296]{2,1,0:T(1,128)}, u32[]{:S(2)}, u32[]{:S(2)}) async-start(f32[4,1,55296]{2,1,0:T(1,128)} %reshape.171), calls=%async_computation.4 | async-start | bytes 1769472 | tf_op jit(solution)/shard_map/all_to_all | solution.py:88
  410.8 4.6 copy-start.6
  410.8 17.9 %all-to-all-start.13 = ((f32[4,1,55296]{2,1,0:T(1,128)}), f32[4,1,55296]{2,1,0:T(1,128)}, u32[]{:S(2)}, u32[]{:S(2)}) async-start(f32[4,1,55296]{2,1,0:T(1,128)} %reshape.165), calls=%async_computation.13 | async-start | bytes 1769472 | tf_op jit(solution)/shard_map/all_to_all | solution.py:89
  428.7 46.7 %all-to-all-start.12 = ((f32[4,1,55296]{2,1,0:T(1,128)}), f32[4,1,55296]{2,1,0:T(1,128)}, u32[]{:S(2)}, u32[]{:S(2)}) async-start(f32[4,1,55296]{2,1,0:T(1,128)} %reshape.163), calls=%async_computation.12 | async-start | bytes 1769472 | tf_op jit(solution)/shard_map/all_to_all | solution.py:88
  475.5 32.0 %all-to-all-start.7 = ((f32[192,12,96]{2,1,0:T(8,128)}), f32[192,12,96]{2,1,0:T(8,128)}, u32[]{:S(2)}, u32[]{:S(2)}) async-start(f32[192,12,96]{2,1,0:T(8,128)} %copy.223), calls=%async_computation.7 | async-start | bytes 3145728 | tf_op jit(solution)/shard_map/all_to_all | solution.py:103
  507.4 47.5 %all-to-all-start.6 = ((f32[192,12,96]{2,1,0:T(8,128)}), f32[192,12,96]{2,1,0:T(8,128)}, u32[]{:S(2)}, u32[]{:S(2)}) async-start(f32[192,12,96]{2,1,0:T(8,128)} %copy.218), calls=%async_computation.6 | async-start | bytes 3145728 | tf_op jit(solution)/shard_map/all_to_all | solution.py:102
  554.9 30.2 %all-to-all-start.15 = ((f32[192,12,96]{2,1,0:T(8,128)}), f32[192,12,96]{2,1,0:T(8,128)}, u32[]{:S(2)}, u32[]{:S(2)}) async-start(f32[192,12,96]{2,1,0:T(8,128)} %copy.259), calls=%async_computation.15 | async-start | bytes 3145728 | tf_op jit(solution)/shard_map/all_to_all | solution.py:103
  570.2 20.0 %copy-start.19 = (s32[4]{0:T(128)S(1)}, s32[4]{0:T(128)}, u32[]{:S(2)}) copy-start(s32[4]{0:T(128)} %param.7) | copy-start | bytes 52
  585.2 27.6 %all-to-all-start.14 = ((f32[192,12,96]{2,1,0:T(8,128)}), f32[192,12,96]{2,1,0:T(8,128)S(1)}, u32[]{:S(2)}, u32[]{:S(2)}) async-start(f32[192,12,96]{2,1,0:T(8,128)} %copy.254), calls=%async_computation.14 | async-start | bytes 3145728 | tf_op jit(solution)/shard_map/all_to_all | solution.py:102
  (13 other events, 31.5 us)
Sparse Core Ops, SparseCore 0:
  15.6 53.0 all-reduce.2
where the time goes:
time: 640 us; the launch traced here: 631 us
  local copies, waits for them, and re-layouts  240 us (38%)
  waiting for transfers between devices  134 us (21%)
  matrix products  105 us (16%)
  starting transfers between devices  86 us (13%)
  other arithmetic  44.9 us (7%)
  between operations  20.8 us (3%)
    dot_general x32, matrix products, contract(): jnp.einsum(form, left, right, precision=lax.Precision.HIGHEST, preferred_...  87.1 us
    unnamed x56, local copies, waits for them, and re-layouts  81.4 us
    psum x1, waiting for transfers between devices, from_root(): return lax.psum(block, axis)  53.2 us
    all_to_all x2, waiting for transfers between devices, potentials(): lax.all_to_all(near_imag, 'pcol', split_axis=0, concat_axis=1, tiled=True)  30 us
    all_to_all x2, waiting for transfers between devices, potentials(): lax.all_to_all(spec_real, 'pcol', split_axis=0, concat_axis=1, tiled=True)  22.8 us
    all_to_all x2, waiting for transfers between devices, potentials(): lax.all_to_all(spec_imag, 'pcol', split_axis=0, concat_axis=1, tiled=True)  20.4 us
    unnamed x8, matrix products  18.1 us
    all_to_all x2, starting transfers between devices, potentials(): lax.all_to_all(near_imag, 'pcol', split_axis=0, concat_axis=1, tiled=True)  16.2 us
  transfers between devices with their start and end apart: 17, of which 8 were waited for; matrix products, arithmetic and copies ran while one was open for 56% of the time, Pallas kernels for 0%

commit v1 on v0

v1 whole, which is shorter than its diff:
```python
import functools

import jax
import jax.numpy as jnp
import ml_dtypes
import numpy as np
from jax import lax
from jax.experimental import pallas as pl
from jax.experimental.pallas import tpu as pltpu
from jax.sharding import PartitionSpec as P

N = 192
PC = 16
PR = 4
YB = 12
XB = 48
PARTS = 3
K4 = 4
W = 384
CH = 24
F32 = jnp.float32
BF16 = jnp.bfloat16
MESH = pl.DeviceIdType.MESH


def split_table(table):
    high = table.astype(np.float32).astype(ml_dtypes.bfloat16)
    low = (table - high.astype(np.float64)).astype(np.float32).astype(ml_dtypes.bfloat16)
    return high, low


def complex_table(out_part, out_freq, in_part, in_point, sign):
    angle = 2.0 * np.pi * ((out_freq[:, None] * in_point[None, :]) % N) / N
    cosine, sine = np.cos(angle), sign * np.sin(angle)
    op, ip = out_part[:, None], in_part[None, :]
    return np.where(op == ip, cosine, np.where(op == 0, -sine, sine))


def grid(*sizes):
    return [a.reshape(-1) for a in np.meshgrid(*[np.arange(s) for s in sizes], indexing="ij")]


def make_tables():
    z_part = np.concatenate([np.zeros(128), np.ones(128), np.zeros(64), np.ones(64)]).astype(int)
    z_point = np.concatenate([np.arange(128)] * 2 + [np.arange(128, 192)] * 2)
    c, k4, s, q = grid(2, K4, PARTS, PC)
    kz = q * YB + s * K4 + k4
    t1 = complex_table(c, kz, z_part, z_point, -1)
    k4, c, s, q = grid(K4, 2, PARTS, PC)
    kz = q * YB + s * K4 + k4
    t5 = -0.25 * complex_table(z_part, z_point, c, kz, 1).T
    p, y, yc = grid(PC, YB, 2)
    y_point = p * YB + y
    u, uc, k = grid(PR, 2, XB)
    ky = u * XB + k
    t2 = complex_table(uc, ky, yc, y_point, -1).T
    t4 = complex_table(yc, y_point, uc, ky, 1)
    xc, kx = grid(2, N)
    t3 = complex_table(xc, kx, uc, ky, -1)
    t3i = complex_table(uc, ky, xc, kx, 1) / float(N) ** 3
    return [part for t in (t1, t2, t3, t3i, t4, t5) for part in split_table(t)]


def halves(x):
    high = x.astype(BF16)
    return high, (x - high.astype(F32)).astype(BF16)


def dot3(left, right, dims):
    def dot(a, b):
        return lax.dot_general(a, b, (dims, ((), ())), preferred_element_type=F32)

    return dot(left[0], right[0]) + (dot(left[0], right[1]) + dot(left[1], right[0]))


NN = ((1,), (0,))
NT = ((1,), (1,))


def swap_slots(blocks):
    slot = lax.broadcasted_iota(jnp.int32, (XB, W), 1) // XB
    blocks = list(blocks)
    for bit in (1, 2, 4):
        keep = (slot & bit) == 0
        for m in range(8):
            if m & bit == 0:
                a, b = blocks[m], blocks[m + bit]
                blocks[m] = jnp.where(keep, a, pltpu.roll(b, XB * bit, 1))
                blocks[m + bit] = jnp.where(keep, pltpu.roll(a, W - XB * bit, 1), b)
    return blocks


def body(
    c_ref, phi_ref, ker_ref, t1h, t1l, t2h, t2l, t3h, t3l, t3ih, t3il, t4h, t4l, t5h, t5l,
    out_ref,
    psi, s1, r1, s2, r2, s3, r3, s4, r4,
    psi_send, psi_recv, own_sem, send_sem, recv_sem,
):
    me_p = lax.axis_index("pcol")
    me_r = lax.axis_index("prow")
    partner = 1 - lax.axis_index("band")

    barrier = pltpu.get_barrier_semaphore()

    def greet_p(k, _):
        pl.semaphore_signal(barrier, inc=1, device_id={"pcol": lax.rem(me_p + k, PC)}, device_id_type=MESH)
        return 0

    def greet_r(k, _):
        pl.semaphore_signal(barrier, inc=1, device_id={"prow": lax.rem(me_r + k, PR)}, device_id_type=MESH)
        return 0

    lax.fori_loop(1, PC, greet_p, 0)
    lax.fori_loop(1, PR, greet_r, 0)
    pl.semaphore_signal(barrier, inc=1, device_id={"band": partner}, device_id_type=MESH)
    pl.semaphore_wait(barrier, PC - 1 + PR - 1 + 1)

    groups = 3
    rows = YB // groups * XB

    def psi_copy(g):
        return pltpu.make_async_remote_copy(
            src_ref=c_ref.at[pl.ds(g * rows, rows)],
            dst_ref=psi.at[pl.ds(g * rows, rows)],
            send_sem=psi_send.at[g],
            recv_sem=psi_recv.at[g],
            device_id={"band": partner},
            device_id_type=MESH,
        )

    for g in range(groups):
        psi_copy(g).start()

    def pcol_start(e, s, src, dst):
        mine = pl.ds(me_p * CH, CH)

        def send(k, _):
            to = lax.rem(me_p + k, PC)
            pltpu.make_async_remote_copy(
                src_ref=src.at[s, :, pl.ds(to * CH, CH), :],
                dst_ref=dst.at[s, :, mine, :],
                send_sem=send_sem.at[e, s],
                recv_sem=recv_sem.at[e, s],
                device_id={"pcol": to},
                device_id_type=MESH,
            ).start()
            return 0

        lax.fori_loop(1, PC, send, 0)
        pltpu.make_async_copy(src.at[s, :, mine, :], dst.at[s, :, mine, :], own_sem.at[e, s]).start()

    def pcol_wait(e, s, src, dst):
        mine = pl.ds(me_p * CH, CH)
        pltpu.make_async_copy(src.at[s, :, mine, :], dst.at[s, :, mine, :], own_sem.at[e, s]).wait()
        others = dst.at[s, :, pl.ds(0, (PC - 1) * CH), :]
        pltpu.make_async_copy(others, others, recv_sem.at[e, s]).wait()

    def pcol_sent(e, s, src):
        others = src.at[s, :, pl.ds(0, (PC - 1) * CH), :]
        pltpu.make_async_copy(others, others, send_sem.at[e, s]).wait()

    def prow_start(e, s, src, dst):
        def send(k, _):
            to = lax.rem(me_r + k, PR)
            pltpu.make_async_remote_copy(
                src_ref=src.at[s, to],
                dst_ref=dst.at[s, me_r],
                send_sem=send_sem.at[e, s],
                recv_sem=recv_sem.at[e, s],
                device_id={"prow": to},
                device_id_type=MESH,
            ).start()
            return 0

        lax.fori_loop(1, PR, send, 0)
        pltpu.make_async_copy(src.at[s, me_r], dst.at[s, me_r], own_sem.at[e, s]).start()

    def prow_wait(e, s, src, dst):
        pltpu.make_async_copy(src.at[s, me_r], dst.at[s, me_r], own_sem.at[e, s]).wait()
        others = dst.at[s, pl.ds(0, PR - 1)]
        pltpu.make_async_copy(others, others, recv_sem.at[e, s]).wait()

    def prow_sent(e, s, src):
        others = src.at[s, pl.ds(0, PR - 1)]
        pltpu.make_async_copy(others, others, send_sem.at[e, s]).wait()

    def forward_z(y, _):
        at = pl.ds(pl.multiple_of(y * XB, 16), XB)
        source = c_ref[at, :] + psi[at, :]
        psi[at, :] = source
        dens = jnp.concatenate(
            [phi_ref[pl.ds(pl.multiple_of(y * 2 * XB + j * XB, 16), XB), :] * source for j in range(2)], axis=0
        )
        spec = dot3((t1h[...], t1l[...]), halves(dens), NT)
        for c in range(2):
            base = c * K4 * XB
            wide = jnp.concatenate([spec[base + k * XB : base + (k + 1) * XB] for k in range(K4)], axis=1)
            for s in range(PARTS):
                for lane in range(3):
                    s1[s, lane, pl.ds(y * 2 + c, PC, stride=CH), :] = wide[
                        s * PC : (s + 1) * PC, lane * 128 : (lane + 1) * 128
                    ]
        return 0

    for g in range(groups):
        psi_copy(g).wait_recv()
        lax.fori_loop(g * (YB // groups), (g + 1) * (YB // groups), forward_z, 0)
    for s in range(PARTS):
        pcol_start(0, s, s1, r1)

    def forward_y(s):
        pcol_wait(0, s, s1, r1)
        turned = jnp.concatenate([r1[s, lane].T for lane in range(3)], axis=0)
        spec = dot3(halves(turned), (t2h[...], t2l[...]), NN)
        spec = swap_slots([spec[m * XB : (m + 1) * XB] for m in range(8)])
        for w in range(8):
            s2[s, w // 2, (w % 2) * XB : (w % 2 + 1) * XB, :] = spec[w]
        prow_start(1, s, s2, r2)

    def middle_x(s):
        prow_wait(1, s, s2, r2)
        data = r2[s].reshape(W, W)
        freq = dot3((t3h[...], t3l[...]), halves(data), NN)
        weight = ker_ref[s]
        freq = jnp.concatenate([freq[:N] * weight, freq[N:] * weight], axis=0)
        back = dot3((t3ih[...], t3il[...]), halves(freq), NN)
        s3[s] = back.reshape(PR, 2 * XB, W)
        prow_start(2, s, s3, r3)

    def backward_y(s):
        prow_wait(2, s, s3, r3)
        data = swap_slots([r3[s, w // 2, (w % 2) * XB : (w % 2 + 1) * XB, :] for w in range(8)])
        data = jnp.concatenate(data, axis=0)
        back = dot3((t4h[...], t4l[...]), halves(data), NT)
        for lane in range(3):
            s4[s, lane] = back[:, lane * 128 : (lane + 1) * 128]
        pcol_start(3, s, s4, r4)

    forward_y(0)
    forward_y(1)
    middle_x(0)
    forward_y(2)
    middle_x(1)
    backward_y(0)
    middle_x(2)
    backward_y(1)
    backward_y(2)
    for s in range(PARTS):
        pcol_wait(3, s, s4, r4)

    def backward_z(y, _):
        near = jnp.concatenate(
            [
                jnp.concatenate([r4[s, lane, pl.ds(y * 2 + c, PC, stride=CH), :] for lane in range(3)], axis=1)
                for c in range(2)
                for s in range(PARTS)
            ],
            axis=0,
        )
        lhs = jnp.concatenate([near[:, k * 2 * XB : (k + 1) * 2 * XB] for k in range(K4)], axis=0)
        lhs = jnp.concatenate([lhs, jnp.zeros((W, 32), F32)], axis=1)
        field = dot3(halves(lhs.T[: 2 * XB]), (t5h[...], t5l[...]), NN)
        source = psi[pl.ds(pl.multiple_of(y * XB, 16), XB), :]
        for j in range(2):
            term = field[j * XB : (j + 1) * XB] * source
            rest = term[:, 256:]
            at = pl.ds(pl.multiple_of(y * 2 * XB + j * XB, 16), XB)
            out_ref[at, :128] = term[:, :128] + term[:, 128:256]
            out_ref[at, 128:] = (rest + pltpu.roll(rest, 64, 1))[:, :64]
        return 0

    lax.fori_loop(0, YB, backward_z, 0)
    for g in range(groups):
        psi_copy(g).wait_send()
    for s in range(PARTS):
        pcol_sent(0, s, s1)
        prow_sent(1, s, s2)
        prow_sent(2, s, s3)
        pcol_sent(3, s, s4)


def spread(a):
    return jnp.concatenate([a[..., :128], a[..., :128], a[..., 128:], a[..., 128:]], axis=-1)


def on_device(orbitals, kernel, plan, occupation):
    laid = jnp.transpose(orbitals, (2, 0, 1, 3))
    group = lax.axis_index("band")
    own = []
    for r in range(2):
        block = plan[r]
        occupied = lax.dynamic_index_in_dim(occupation, block, 0, keepdims=False) != 0
        mine = jnp.logical_and(block // 2 == group, occupied)
        band = lax.dynamic_index_in_dim(laid, block % 2, 1, keepdims=False)
        own.append(jnp.where(mine, band, jnp.zeros_like(band)))
    c = jnp.concatenate([own[0][..., :128], own[1][..., :128], own[0][..., 128:], own[1][..., 128:]], axis=-1)
    c = c.reshape(YB * XB, W)
    phi = spread(laid).reshape(YB * 2 * XB, W)
    ker = jnp.transpose(kernel.reshape(XB, PARTS, K4, N), (1, 3, 2, 0))
    ker = jnp.broadcast_to(ker[:, :, :, None, :], (PARTS, N, K4, 2, XB)).reshape(PARTS, N, W)
    tables = [jnp.asarray(t) for t in make_tables()]
    pcol_buf = pltpu.VMEM((PARTS, 3, PC * CH, 128), F32)
    prow_buf = pltpu.VMEM((PARTS, PR, 2 * XB, W), F32)
    vmem = pl.BlockSpec(memory_space=pltpu.VMEM)
    out = pl.pallas_call(
        body,
        out_shape=jax.ShapeDtypeStruct((YB * 2 * XB, N), F32),
        in_specs=[vmem] * 15,
        out_specs=vmem,
        scratch_shapes=[
            pltpu.VMEM((YB * XB, W), F32),
            pcol_buf, pcol_buf, prow_buf, prow_buf, prow_buf, prow_buf, pcol_buf, pcol_buf,
            pltpu.SemaphoreType.DMA((3,)),
            pltpu.SemaphoreType.DMA((3,)),
            pltpu.SemaphoreType.DMA((4, PARTS)),
            pltpu.SemaphoreType.DMA((4, PARTS)),
            pltpu.SemaphoreType.DMA((4, PARTS)),
        ],
        compiler_params=pltpu.CompilerParams(
            collective_id=0, has_side_effects=True, vmem_limit_bytes=56 * 2**20
        ),
    )(c, phi, ker, *tables)
    return jnp.transpose(out.reshape(YB, 2, XB, N), (1, 2, 0, 3))


def solution(mesh):
    return jax.shard_map(
        on_device,
        mesh=mesh,
        in_specs=(P("band", "prow", "pcol", None), P("prow", "pcol", None), P(), P()),
        out_specs=P("band", "prow", "pcol", None),
        check_vma=False,
    )
```

time: 640 us -> 126 us (0.20); the launches traced: 631 us -> 126 us
  local copies, waits for them, and re-layouts: 240 us -> 10.2 us
  waiting for transfers between devices: 134 us -> 0 us
  matrix products: 105 us -> 0 us
  Pallas kernels: 0 us -> 105 us
  starting transfers between devices: 86 us -> 0 us
  other arithmetic: 44.9 us -> 1.4 us
  between operations: 20.8 us -> 9.02 us
    pallas_call x0 -> x1, Pallas kernels: none -> 105 us  [on_device(): pl.pallas_call(body, out_shape=jax.ShapeDtypeStruct((YB * 2 * XB, N), F32...]
    dot_general x32 -> x0, matrix products: 87.1 us -> none  [contract(): jnp.einsum(form, left, right, precision=lax.Precision.HIGHEST, preferred_...]
    all_to_all x16 -> x0, starting transfers between devices: 86 us -> none  [the longest x2 16.2 us: potentials(): lax.all_to_all(near_imag, 'pcol', split_axis=0, concat_axis=1, tiled=True)]
    unnamed x56 -> x4, local copies, waits for them, and re-layouts: 81.4 us -> 0.01 us
    all_to_all x16 -> x0, waiting for transfers between devices: 80.7 us -> none  [the longest x2 30 us: potentials(): lax.all_to_all(near_imag, 'pcol', split_axis=0, concat_axis=1, tiled=True)]
    reshape x26 -> x2, local copies, waits for them, and re-layouts: 75.4 us -> 3.66 us  [the longest x1 2.38 us: on_device(): return jnp.transpose(out.reshape(YB, 2, XB, N), (1, 2, 0, 3))]
    all_to_all x29 -> x0, local copies, waits for them, and re-layouts: 59.3 us -> none  [the longest x6 13.7 us: potentials(): lax.all_to_all(spec_real, 'pcol', split_axis=0, concat_axis=1, tiled=True)]
    psum x1 -> x0, waiting for transfers between devices: 53.2 us -> none  [from_root(): return lax.psum(block, axis)]
  transfers between devices with their start and end apart: 17 -> 0, of which waited for: 8 -> 0; matrix products, arithmetic and copies ran while one was open for 56% -> 0% of each run, Pallas kernels for 0% -> 0%
where the time goes in v1:
time: 126 us
  Pallas kernels  105 us (83%)
  local copies, waits for them, and re-layouts  10.2 us (8%)
  between operations  9.02 us (7%)
  other arithmetic  1.4 us (1%)
    pallas_call x1, Pallas kernels, on_device(): pl.pallas_call(body, out_shape=jax.ShapeDtypeStruct((YB * 2 * XB, N), F32...  105 us

profile of v1, /device:TPU:1, one launch (start us, length us, event | category | flops | bytes accessed | tf_op | source)
XLA Modules:
  0.0 125.8 jit_solution(16274648807868609564)
XLA Ops:
  0.0 0.0 copy-start
  0.0 1.4 %fusion.1 = (s32[1]{0:T(128)}, s32[1]{0:T(128)}) fusion(s32[4]{0:T(128)} %param.18), kind=kLoop, calls=%fused_computation.6 | loop fusion | bytes 16 | tf_op jit(solution)/shard_map/slice | solution.py:291
  9.0 1.3 %fusion = (s32[1]{0:T(128)}, s32[1]{0:T(128)}) fusion(s32[4]{0:T(128)} %param.19, s32[]{:T(128)S(6)} %select_n.59, s32[]{:T(128)S(6)} %select_n.67), kind=kLoop, calls=%fused_computation.5 | loop fusion | bytes 24 | tf_op jit(solution)/shard_map/jit(dynamic_index_in_dim)/dynamic_slice | solution.py:292
  11.6 1.1 slice.40
  12.7 1.1 slice.39
  13.8 0.0 copy-done
  13.9 0.3 pad_maximum_fusion
  14.1 1.4 %copy.20 = f32[12,2,48,384]{3,2,1,0:T(8,128)} copy(f32[12,2,48,384]{3,2,0,1:T(8,128)S(1)} %pad_maximum_fusion) | data formatting | bytes 3538944 | tf_op jit(solution)/shard_map/concatenate | solution.py:283
  15.5 0.1 select_bitcast_fusion.1
  15.7 0.0 copy-start.1
  15.7 1.1 pad_maximum_fusion.1
  16.8 0.0 copy-done.1
  16.8 0.1 broadcast_in_dim.2
  16.9 1.3 %copy.21.ker_ref = f32[3,192,384]{2,1,0:T(8,128)} copy(f32[3,192,384]{1,2,0:T(8,128)S(1)} %bitcast.27) | data formatting | bytes 1769472 | tf_op jit(solution)/shard_map/reshape | solution.py:300
  18.2 105.2 %shard_map.154 = f32[1152,192]{1,0:T(8,128)} custom-call(f32[576,384]{1,0:T(8,128)} %bitcast.29, f32[1152,384]{1,0:T(8,128)} %bitcast.26, f32[3,192,384]{2,1,0:T(8,128)} %copy.21.ker_ref, bf16[384,384]{1,0:T(8,128)(2,1)} %constant.80.clone.t1h, bf16[384,384]{1,0:T(8,128)(2,1)} %constant.81.clone.t1l, bf16[384,384]{1,0:T(8,128)(2,1)} %constant.82.clone.t2h.t4h, ...), custom_call_target="tpu_custom_call" | custom-call | tf_op jit(solution)/shard_map/pallas_call | solution.py:305
  123.5 2.4 %copy.24 = f32[12,2,48,192]{3,2,0,1:T(8,128)} copy(f32[12,2,48,192]{3,2,1,0:T(8,128)} %bitcast.28) | data formatting | bytes 1769472 | tf_op jit(solution)/shard_map/reshape | solution.py:323
  (4 shorter events, 0.1 us)
Async XLA Ops:
  0.0 13.8 %copy-start = (f32[2,48,12,192]{3,1,2,0:T(8,128)S(1)}, f32[2,48,12,192]{3,1,2,0:T(8,128)}, u32[]{:S(2)}) copy-start(f32[2,48,12,192]{3,1,2,0:T(8,128)} %param.16) | copy-start | bytes 2654212
  15.7 1.1 copy-start.1

commit v2 on v1

--- a/solution.py
+++ b/solution.py
@@ -91,14 +91,29 @@
 
 
 def body(
-    c_ref, phi_ref, ker_ref, t1h, t1l, t2h, t2l, t3h, t3l, t3ih, t3il, t4h, t4l, t5h, t5l,
+    plan_ref, occ_ref, orb_hbm, ker_hbm, tables_hbm,
     out_ref,
-    psi, s1, r1, s2, r2, s3, r3, s4, r4,
-    psi_send, psi_recv, own_sem, send_sem, recv_sem,
+    orb, ker, weight, tables, mine, psi, s1, r1, s2, r2, s3, r3, s4, r4,
+    load_sem, psi_send, psi_recv, own_sem, send_sem, recv_sem,
 ):
+    def table(t):
+        return tables[2 * t], tables[2 * t + 1]
+
+    loads = [pltpu.make_async_copy(orb_hbm, orb, load_sem.at[0])]
+    loads += [
+        pltpu.make_async_copy(
+            tables_hbm.at[pl.ds(2 * t, 2)], tables.at[pl.ds(2 * t, 2)], load_sem.at[2 + t]
+        )
+        for t in range(6)
+    ]
+    loads.append(pltpu.make_async_copy(ker_hbm, ker, load_sem.at[1]))
+    for load in loads:
+        load.start()
+
     me_p = lax.axis_index("pcol")
     me_r = lax.axis_index("prow")
-    partner = 1 - lax.axis_index("band")
+    me_b = lax.axis_index("band")
+    partner = 1 - me_b
 
     barrier = pltpu.get_barrier_semaphore()
 
@@ -120,7 +135,7 @@
 
     def psi_copy(g):
         return pltpu.make_async_remote_copy(
-            src_ref=c_ref.at[pl.ds(g * rows, rows)],
+            src_ref=mine.at[pl.ds(g * rows, rows)],
             dst_ref=psi.at[pl.ds(g * rows, rows)],
             send_sem=psi_send.at[g],
             recv_sem=psi_recv.at[g],
@@ -128,8 +143,31 @@
             device_id_type=MESH,
         )
 
+    share = [
+        [
+            jnp.where(
+                jnp.logical_and(plan_ref[r] == 2 * me_b + b, occ_ref[2 * me_b + b] != 0),
+                jnp.float32(1.0), jnp.float32(0.0),
+            )
+            for b in range(2)
+        ]
+        for r in range(2)
+    ]
+
+    def own_source(y, _):
+        at = pl.ds(pl.multiple_of(y * XB, 16), XB)
+        bands = [orb[b, at, :] for b in range(2)]
+        parts = [share[r][0] * bands[0] + share[r][1] * bands[1] for r in range(2)]
+        mine[at, :128] = parts[0][:, :128]
+        mine[at, 128:256] = parts[1][:, :128]
+        mine[at, 256:] = jnp.concatenate([parts[0][:, 128:], parts[1][:, 128:]], axis=1)
+        return 0
+
+    loads[0].wait()
     for g in range(groups):
+        lax.fori_loop(g * (YB // groups), (g + 1) * (YB // groups), own_source, 0)
         psi_copy(g).start()
+    loads[1].wait()
 
     def pcol_start(e, s, src, dst):
         mine = pl.ds(me_p * CH, CH)
@@ -186,12 +224,10 @@
 
     def forward_z(y, _):
         at = pl.ds(pl.multiple_of(y * XB, 16), XB)
-        source = c_ref[at, :] + psi[at, :]
+        source = mine[at, :] + psi[at, :]
         psi[at, :] = source
-        dens = jnp.concatenate(
-            [phi_ref[pl.ds(pl.multiple_of(y * 2 * XB + j * XB, 16), XB), :] * source for j in range(2)], axis=0
-        )
-        spec = dot3((t1h[...], t1l[...]), halves(dens), NT)
+        dens = jnp.concatenate([spread(orb[j, at, :]) * source for j in range(2)], axis=0)
+        spec = dot3(table(0), halves(dens), NT)
         for c in range(2):
             base = c * K4 * XB
             wide = jnp.concatenate([spec[base + k * XB : base + (k + 1) * XB] for k in range(K4)], axis=1)
@@ -207,11 +243,16 @@
         lax.fori_loop(g * (YB // groups), (g + 1) * (YB // groups), forward_z, 0)
     for s in range(PARTS):
         pcol_start(0, s, s1, r1)
+    for load in loads[2:]:
+        load.wait()
+    for s in range(PARTS):
+        block = jnp.concatenate([ker[s * K4 + m // 2] for m in range(8)], axis=0)
+        weight[s] = jnp.concatenate([block, jnp.zeros((W, 64), F32)], axis=1).T[:N]
 
     def forward_y(s):
         pcol_wait(0, s, s1, r1)
         turned = jnp.concatenate([r1[s, lane].T for lane in range(3)], axis=0)
-        spec = dot3(halves(turned), (t2h[...], t2l[...]), NN)
+        spec = dot3(halves(turned), table(1), NN)
         spec = swap_slots([spec[m * XB : (m + 1) * XB] for m in range(8)])
         for w in range(8):
             s2[s, w // 2, (w % 2) * XB : (w % 2 + 1) * XB, :] = spec[w]
@@ -220,10 +261,9 @@
     def middle_x(s):
         prow_wait(1, s, s2, r2)
         data = r2[s].reshape(W, W)
-        freq = dot3((t3h[...], t3l[...]), halves(data), NN)
-        weight = ker_ref[s]
-        freq = jnp.concatenate([freq[:N] * weight, freq[N:] * weight], axis=0)
-        back = dot3((t3ih[...], t3il[...]), halves(freq), NN)
+        freq = dot3(table(2), halves(data), NN)
+        freq = jnp.concatenate([freq[:N] * weight[s], freq[N:] * weight[s]], axis=0)
+        back = dot3(table(3), halves(freq), NN)
         s3[s] = back.reshape(PR, 2 * XB, W)
         prow_start(2, s, s3, r3)
 
@@ -231,7 +271,7 @@
         prow_wait(2, s, s3, r3)
         data = swap_slots([r3[s, w // 2, (w % 2) * XB : (w % 2 + 1) * XB, :] for w in range(8)])
         data = jnp.concatenate(data, axis=0)
-        back = dot3((t4h[...], t4l[...]), halves(data), NT)
+        back = dot3(table(4), halves(data), NT)
         for lane in range(3):
             s4[s, lane] = back[:, lane * 128 : (lane + 1) * 128]
         pcol_start(3, s, s4, r4)
@@ -259,14 +299,14 @@
         )
         lhs = jnp.concatenate([near[:, k * 2 * XB : (k + 1) * 2 * XB] for k in range(K4)], axis=0)
         lhs = jnp.concatenate([lhs, jnp.zeros((W, 32), F32)], axis=1)
-        field = dot3(halves(lhs.T[: 2 * XB]), (t5h[...], t5l[...]), NN)
+        field = dot3(halves(lhs.T[: 2 * XB]), table(5), NN)
         source = psi[pl.ds(pl.multiple_of(y * XB, 16), XB), :]
         for j in range(2):
             term = field[j * XB : (j + 1) * XB] * source
             rest = term[:, 256:]
-            at = pl.ds(pl.multiple_of(y * 2 * XB + j * XB, 16), XB)
-            out_ref[at, :128] = term[:, :128] + term[:, 128:256]
-            out_ref[at, 128:] = (rest + pltpu.roll(rest, 64, 1))[:, :64]
+            at = pl.ds(pl.multiple_of(y * XB, 16), XB)
+            out_ref[j, at, :128] = term[:, :128] + term[:, 128:256]
+            out_ref[j, at, 128:] = (rest + pltpu.roll(rest, 64, 1))[:, :64]
         return 0
 
     lax.fori_loop(0, YB, backward_z, 0)
@@ -284,32 +324,26 @@
 
 
 def on_device(orbitals, kernel, plan, occupation):
-    laid = jnp.transpose(orbitals, (2, 0, 1, 3))
-    group = lax.axis_index("band")
-    own = []
-    for r in range(2):
-        block = plan[r]
-        occupied = lax.dynamic_index_in_dim(occupation, block, 0, keepdims=False) != 0
-        mine = jnp.logical_and(block // 2 == group, occupied)
-        band = lax.dynamic_index_in_dim(laid, block % 2, 1, keepdims=False)
-        own.append(jnp.where(mine, band, jnp.zeros_like(band)))
-    c = jnp.concatenate([own[0][..., :128], own[1][..., :128], own[0][..., 128:], own[1][..., 128:]], axis=-1)
-    c = c.reshape(YB * XB, W)
-    phi = spread(laid).reshape(YB * 2 * XB, W)
-    ker = jnp.transpose(kernel.reshape(XB, PARTS, K4, N), (1, 3, 2, 0))
-    ker = jnp.broadcast_to(ker[:, :, :, None, :], (PARTS, N, K4, 2, XB)).reshape(PARTS, N, W)
-    tables = [jnp.asarray(t) for t in make_tables()]
+    orb = jnp.transpose(orbitals, (0, 2, 1, 3)).reshape(2, YB * XB, N)
+    ker = jnp.transpose(kernel, (1, 0, 2))
+    tables = jnp.asarray(np.stack(make_tables()))
     pcol_buf = pltpu.VMEM((PARTS, 3, PC * CH, 128), F32)
     prow_buf = pltpu.VMEM((PARTS, PR, 2 * XB, W), F32)
     vmem = pl.BlockSpec(memory_space=pltpu.VMEM)
     out = pl.pallas_call(
         body,
-        out_shape=jax.ShapeDtypeStruct((YB * 2 * XB, N), F32),
-        in_specs=[vmem] * 15,
+        out_shape=jax.ShapeDtypeStruct((2, YB * XB, N), F32),
+        in_specs=[pl.BlockSpec(memory_space=pltpu.SMEM)] * 2 + [pl.BlockSpec(memory_space=pl.ANY)] * 3,
         out_specs=vmem,
         scratch_shapes=[
+            pltpu.VMEM((2, YB * XB, N), F32),
+            pltpu.VMEM((YB, XB, N), F32),
+            pltpu.VMEM((PARTS, N, W), F32),
+            pltpu.VMEM((12, W, W), BF16),
+            pltpu.VMEM((YB * XB, W), F32),
             pltpu.VMEM((YB * XB, W), F32),
             pcol_buf, pcol_buf, prow_buf, prow_buf, prow_buf, prow_buf, pcol_buf, pcol_buf,
+            pltpu.SemaphoreType.DMA((8,)),
             pltpu.SemaphoreType.DMA((3,)),
             pltpu.SemaphoreType.DMA((3,)),
             pltpu.SemaphoreType.DMA((4, PARTS)),
@@ -319,8 +353,8 @@
         compiler_params=pltpu.CompilerParams(
             collective_id=0, has_side_effects=True, vmem_limit_bytes=56 * 2**20
         ),
-    )(c, phi, ker, *tables)
-    return jnp.transpose(out.reshape(YB, 2, XB, N), (1, 2, 0, 3))
+    )(plan, occupation, orb, ker, tables)
+    return jnp.transpose(out.reshape(2, YB, XB, N), (0, 2, 1, 3))
 
 
 def solution(mesh):

time: 126 us -> 106 us (0.84)
  between operations: 9.02 us -> 0.01 us
  local copies, waits for them, and re-layouts: 10.2 us -> 2.37 us
  other arithmetic: 1.4 us -> 0 us
    reshape x2 -> x0, local copies, waits for them, and re-layouts: 3.66 us -> none  [the longest x1 2.38 us: on_device(): return jnp.transpose(out.reshape(YB, 2, XB, N), (1, 2, 0, 3))]
    slice x7 -> x0, local copies, waits for them, and re-layouts: 3.65 us -> none  [the longest x1 1.36 us: on_device(): block = plan[r]]
    unnamed x4 -> x1, local copies, waits for them, and re-layouts: 0.01 us -> 2.37 us
    pallas_call x1, Pallas kernels: 105 us -> 104 us  [on_device(): pl.pallas_call(body, out_shape=jax.ShapeDtypeStruct((2, YB * XB, N), F32)...]
    concatenate x1 -> x0, local copies, waits for them, and re-layouts: 1.4 us -> none  [spread(): jnp.concatenate([a[..., :128], a[..., :128], a[..., 128:], a[..., 128:]],...]
    dynamic_slice x1 -> x0, local copies, waits for them, and re-layouts: 1.33 us -> none  [on_device(): lax.dynamic_index_in_dim(occupation, block, 0, keepdims=False) != 0]
    concatenate x2 -> x0, other arithmetic: 1.31 us -> none  [the longest x1 1.06 us: on_device(): jnp.concatenate([own[0][..., :128], own[1][..., :128], own[0][..., 128:],...]
where the time goes in v2:
time: 106 us
  Pallas kernels  104 us (98%)
  local copies, waits for them, and re-layouts  2.37 us (2%)
    pallas_call x1, Pallas kernels, on_device(): pl.pallas_call(body, out_shape=jax.ShapeDtypeStruct((2, YB * XB, N), F32)...  104 us
    unnamed x1, local copies, waits for them, and re-layouts  2.37 us

profile of v2, /device:TPU:1, one launch (start us, length us, event | category | flops | bytes accessed | tf_op | source)
XLA Modules:
  0.0 105.9 jit_solution(8132817169306083964)
XLA Ops:
  0.0 103.6 %shard_map.55 = f32[2,576,192]{2,1,0:T(8,128)} custom-call(s32[4]{0:T(128)} %plan_ref.1, s32[4]{0:T(128)} %occ_ref.1, f32[2,576,192]{2,1,0:T(8,128)} %bitcast.8, f32[12,48,192]{2,1,0:T(8,128)} %bitcast.9, bf16[12,384,384]{2,1,0:T(8,128)(2,1)} %constant.2.clone.tables_hbm), custom_call_target="tpu_custom_call" | custom-call | tf_op jit(solution)/shard_map/pallas_call | solution.py:333
  103.6 2.4 %copy.7 = f32[2,48,12,192]{3,1,2,0:T(8,128)} copy(f32[2,48,12,192]{3,1,2,0:T(8,128)} %bitcast.7) | data formatting | bytes 1769472

commit v3 on v2

v3 whole, which is shorter than its diff:
```python
import functools

import jax
import jax.numpy as jnp
import ml_dtypes
import numpy as np
from jax import lax
from jax.experimental import pallas as pl
from jax.experimental.pallas import tpu as pltpu
from jax.sharding import PartitionSpec as P

N = 192
PC = 16
PR = 4
YB = 12
XB = 48
PARTS = 3
K4 = 4
CUTS = 3
XC = 16
W = 384
CH = 24
F32 = jnp.float32
BF16 = jnp.bfloat16
MESH = pl.DeviceIdType.MESH


def split_table(table):
    high = table.astype(np.float32).astype(ml_dtypes.bfloat16)
    low = (table - high.astype(np.float64)).astype(np.float32).astype(ml_dtypes.bfloat16)
    return high, low


def complex_table(out_part, out_freq, in_part, in_point, sign):
    angle = 2.0 * np.pi * ((out_freq[:, None] * in_point[None, :]) % N) / N
    cosine, sine = np.cos(angle), sign * np.sin(angle)
    op, ip = out_part[:, None], in_part[None, :]
    return np.where(op == ip, cosine, np.where(op == 0, -sine, sine))


def grid(*sizes):
    return [a.reshape(-1) for a in np.meshgrid(*[np.arange(s) for s in sizes], indexing="ij")]


def make_tables():
    z_part = np.concatenate([np.zeros(128), np.ones(128), np.zeros(64), np.ones(64)]).astype(int)
    z_point = np.concatenate([np.arange(128)] * 2 + [np.arange(128, 192)] * 2)
    k4, c, s, q = grid(K4, 2, PARTS, PC)
    kz = q * YB + s * K4 + k4
    t1 = complex_table(c, kz, z_part, z_point, -1)
    t5 = -0.25 * complex_table(z_part, z_point, c, kz, 1).T
    p, y, yc = grid(PC, YB, 2)
    y_point = p * YB + y
    u, uc, k = grid(PR, 2, XB)
    ky = u * XB + k
    t2 = complex_table(uc, ky, yc, y_point, -1).T
    t4 = complex_table(yc, y_point, uc, ky, 1)
    xc, kx = grid(2, N)
    v, cut, vc, x = grid(PR, CUTS, 2, XC)
    x_point = v * XB + cut * XC + x
    t3 = complex_table(xc, kx, vc, x_point, -1)
    t3i = complex_table(vc, x_point, xc, kx, 1) / float(N) ** 3
    return [part for t in (t1, t2, t3, t3i, t4, t5) for part in split_table(t)]


def halves(x):
    high = x.astype(BF16)
    return high, (x - high.astype(F32)).astype(BF16)


def dot3(left, right, dims):
    def dot(a, b):
        return lax.dot_general(a, b, (dims, ((), ())), preferred_element_type=F32)

    return dot(left[0], right[0]) + (dot(left[0], right[1]) + dot(left[1], right[0]))


NN = ((1,), (0,))
NT = ((1,), (1,))


def swap_slots(blocks, width):
    count = len(blocks)
    lanes = count * width
    slot = lax.broadcasted_iota(jnp.int32, blocks[0].shape, 1) // width
    blocks = list(blocks)
    bit = 1
    while bit < count:
        keep = (slot & bit) == 0
        for m in range(count):
            if m & bit == 0:
                a, b = blocks[m], blocks[m + bit]
                blocks[m] = jnp.where(keep, a, pltpu.roll(b, width * bit, 1))
                blocks[m + bit] = jnp.where(keep, pltpu.roll(a, lanes - width * bit, 1), b)
        bit *= 2
    return blocks


def body(
    plan_ref, occ_ref, orb_hbm, ker_hbm, tables_hbm,
    out_ref,
    orb, ker, weight, tables, mine, other, psi, s1, r1, s2, r2, s3, r3, s4, r4,
    load_sem, psi_send, psi_recv, own_sem, send_sem, recv_sem,
):
    def table(t):
        return tables[2 * t], tables[2 * t + 1]

    me_p = lax.axis_index("pcol")
    me_r = lax.axis_index("prow")
    me_b = lax.axis_index("band")
    half = lax.rem(me_p // 2, 2)
    work = lax.rem(me_b + half, 2)
    partner = 1 - me_b

    barrier = pltpu.get_barrier_semaphore()

    def greet_p(k, _):
        to = lax.rem(me_p * 2 + me_b + k, 2 * PC)
        pl.semaphore_signal(
            barrier, inc=1, device_id={"pcol": to // 2, "band": lax.rem(to, 2)}, device_id_type=MESH
        )
        return 0

    def greet_r(k, _):
        pl.semaphore_signal(barrier, inc=1, device_id={"prow": lax.rem(me_r + k, PR)}, device_id_type=MESH)
        return 0

    loads = [
        pltpu.make_async_copy(orb_hbm.at[:, :, pl.ds(cut * XC, XC), :], orb.at[cut], load_sem.at[cut])
        for cut in range(CUTS)
    ]
    loads += [
        pltpu.make_async_copy(
            tables_hbm.at[pl.ds(2 * t, 2)], tables.at[pl.ds(2 * t, 2)], load_sem.at[4 + t]
        )
        for t in range(6)
    ]
    loads.append(pltpu.make_async_copy(ker_hbm, ker, load_sem.at[3]))
    for load in loads[: CUTS + 1]:
        load.start()
    lax.fori_loop(1, 2 * PC, greet_p, 0)
    lax.fori_loop(1, PR, greet_r, 0)

    rows = YB * XC

    def band_copy(cut):
        return pltpu.make_async_remote_copy(
            src_ref=mine.at[pl.ds(cut * rows, rows)],
            dst_ref=other.at[pl.ds(cut * rows, rows)],
            send_sem=psi_send.at[cut],
            recv_sem=psi_recv.at[cut],
            device_id={"band": partner},
            device_id_type=MESH,
        )

    for cut in range(CUTS):
        loads[cut].wait()
        for y in range(YB):
            at = pl.ds(cut * rows + y * XC, XC)
            mine[at, :128] = orb[cut, 0, y, :, :128]
            mine[at, 128:256] = orb[cut, 1, y, :, :128]
            mine[at, 256:] = jnp.concatenate([orb[cut, 0, y, :, 128:], orb[cut, 1, y, :, 128:]], axis=1)
        if cut == 0:
            pl.semaphore_wait(barrier, 2 * PC - 1 + PR - 1)
        band_copy(cut).start()
    for load in loads[CUTS + 1 :]:
        load.start()

    share = [
        [
            [
                jnp.where(
                    jnp.logical_and(plan_ref[r] == 2 * owner + t, occ_ref[2 * owner + t] != 0),
                    jnp.float32(1.0), jnp.float32(0.0),
                )
                for t in range(2)
            ]
            for owner in (me_b, partner)
        ]
        for r in range(2)
    ]
    first_half = lax.broadcasted_iota(jnp.int32, (XC, 128), 1) < 64
    straight = [jnp.where(first_half, share[0][g][0], share[1][g][1]) for g in range(2)]
    crossed = [jnp.where(first_half, share[0][g][1], share[1][g][0]) for g in range(2)]

    def pair_density(at):
        tiles = []
        for ref in (mine, other):
            high = ref[at, 256:]
            tiles.append((ref[at, :128], ref[at, 128:256], high, pltpu.roll(high, 64, 1)))
        source = [
            sum(share[r][g][t] * tiles[g][t] for g in range(2) for t in range(2)) for r in range(2)
        ]
        source.append(sum(straight[g] * tiles[g][2] + crossed[g] * tiles[g][3] for g in range(2)))
        for n in range(3):
            psi[at, n * 128 : (n + 1) * 128] = source[n]
        low0, low1, high, turned = [jnp.where(half == 1, b, a) for a, b in zip(*tiles)]
        phi = [(low0, jnp.where(first_half, high, turned)), (low1, jnp.where(first_half, turned, high))]
        return [
            jnp.concatenate([low * source[0], low * source[1], up * source[2]], axis=1) for low, up in phi
        ]

    def pcol_start(e, s, cut, src, dst):
        here = pl.ds(me_p * CH, CH)

        def send(k, _):
            to = lax.rem(me_p + k, PC)
            band = lax.rem(work + lax.rem(to // 2, 2), 2) if e == 0 else work
            pltpu.make_async_remote_copy(
                src_ref=src.at[s, cut, pl.ds(to * CH, CH), :],
                dst_ref=dst.at[s, cut, here, :],
                send_sem=send_sem.at[e, s, cut],
                recv_sem=recv_sem.at[e, s, cut],
                device_id={"pcol": to, "band": band},
                device_id_type=MESH,
            ).start()
            return 0

        own = pltpu.make_async_copy(src.at[s, cut, here, :], dst.at[s, cut, here, :], own_sem.at[e, s, cut])
        if e == 0:
            lax.fori_loop(1, PC, send, 0)
            own.start()
        else:
            lax.fori_loop(1 - half, PC, send, 0)
            pl.when(half == 0)(own.start)

    def pcol_all(sem, e, s, cut, ref):
        def wait_for(count):
            part = ref.at[s, cut, pl.ds(0, count * CH), :]
            return pltpu.make_async_copy(part, part, sem.at[e, s, cut]).wait

        if e == 0:
            wait_for(PC - 1)()
        else:
            pl.when(half == 0)(wait_for(PC - 1))
            pl.when(half == 1)(wait_for(PC))

    def pcol_wait(e, s, cut, src, dst):
        here = pl.ds(me_p * CH, CH)
        own = pltpu.make_async_copy(src.at[s, cut, here, :], dst.at[s, cut, here, :], own_sem.at[e, s, cut])
        if e == 0:
            own.wait()
        else:
            pl.when(half == 0)(own.wait)
        pcol_all(recv_sem, e, s, cut, dst)

    def pcol_sent(e, s, cut, src):
        pcol_all(send_sem, e, s, cut, src)

    def prow_start(e, s, cut, src, dst):
        def send(k, _):
            to = lax.rem(me_r + k, PR)
            pltpu.make_async_remote_copy(
                src_ref=src.at[s, to, cut],
                dst_ref=dst.at[s, me_r, cut],
                send_sem=send_sem.at[e, s, cut],
                recv_sem=recv_sem.at[e, s, cut],
                device_id={"prow": to},
                device_id_type=MESH,
            ).start()
            return 0

        lax.fori_loop(1, PR, send, 0)
        pltpu.make_async_copy(src.at[s, me_r, cut], dst.at[s, me_r, cut], own_sem.at[e, s, cut]).start()

    def prow_wait(e, s, cut, src, dst):
        pltpu.make_async_copy(src.at[s, me_r, cut], dst.at[s, me_r, cut], own_sem.at[e, s, cut]).wait()
        others = dst.at[s, pl.ds(0, PR - 1), cut]
        pltpu.make_async_copy(others, others, recv_sem.at[e, s, cut]).wait()

    def prow_sent(e, s, cut, src):
        others = src.at[s, pl.ds(0, PR - 1), cut]
        pltpu.make_async_copy(others, others, send_sem.at[e, s, cut]).wait()

    def forward_z(cut):
        def step(group, _):
            dens = []
            for y4 in range(4):
                y = group * 4 + y4
                dens += pair_density(pl.ds(pl.multiple_of(cut * rows + y * XC, 16), XC))
            spec = dot3(table(0), halves(jnp.concatenate(dens, axis=0)), NT)
            spec = swap_slots([spec[k * 96 : (k + 1) * 96] for k in range(K4)], 32)
            for y4 in range(4):
                for c in range(2):
                    for s in range(PARTS):
                        first = (c * PARTS + s) * PC
                        s1[s, cut, pl.ds((group * 4 + y4) * 2 + c, PC, stride=CH), :] = spec[y4][first : first + PC]
            return 0

        band_copy(cut).wait_recv()
        lax.fori_loop(0, YB // 4, step, 0)
        for s in range(PARTS):
            pcol_start(0, s, cut, s1, r1)

    def forward_y(parts, cut):
        for s in parts:
            pcol_wait(0, s, cut, s1, r1)
        turned = jnp.concatenate([r1[s, cut].T for s in parts], axis=0)
        spec = dot3(halves(turned), table(1), NN)
        for i, s in enumerate(parts):
            blocks = swap_slots([spec[i * 128 + m * XC : i * 128 + (m + 1) * XC] for m in range(8)], XB)
            for w in range(8):
                s2[s, w // 2, cut, (w % 2) * XC : (w % 2 + 1) * XC, :] = blocks[w]
            prow_start(1, s, cut, s2, r2)

    def middle_x(s):
        for cut in range(CUTS):
            prow_wait(1, s, cut, s2, r2)
        data = r2[s].reshape(W, W)
        freq = dot3(table(2), halves(data), NN)
        freq = jnp.concatenate([freq[:N] * weight[s], freq[N:] * weight[s]], axis=0)
        back = dot3(table(3), halves(freq), NN)
        s3[s] = back.reshape(PR, CUTS, 2 * XC, W)
        for cut in range(CUTS):
            prow_start(2, s, cut, s3, r3)

    def backward_y(s, cuts):
        data = []
        for cut in cuts:
            prow_wait(2, s, cut, s3, r3)
            data += swap_slots([r3[s, w // 2, cut, (w % 2) * XC : (w % 2 + 1) * XC, :] for w in range(8)], XB)
        back = dot3(table(4), halves(jnp.concatenate(data, axis=0)), NT)
        for i, cut in enumerate(cuts):
            s4[s, cut] = back[:, i * 128 : (i + 1) * 128]
            pcol_start(3, s, cut, s4, r4)

    def backward_z(cut):
        def step(group, _):
            near = [
                jnp.concatenate(
                    [
                        r4[s, cut, pl.ds((group * 4 + y4) * 2 + c, PC, stride=CH), :]
                        for c in range(2)
                        for s in range(PARTS)
                    ],
                    axis=0,
                )
                for y4 in range(4)
            ]
            near = jnp.concatenate(swap_slots(near, 32), axis=0)
            field = dot3(halves(near.T), table(5), NN)
            for y4 in range(4):
                y = group * 4 + y4
                source = psi[pl.ds(pl.multiple_of(cut * rows + y * XC, 16), XC), :]
                at = pl.ds(pl.multiple_of(y * XB + cut * XC, 16), XC)
                for j in range(2):
                    first = (y4 * 2 + j) * XC
                    term = field[first : first + XC] * source
                    rest = term[:, 256:]
                    out_ref[j, at, :128] = term[:, :128] + term[:, 128:256]
                    out_ref[j, at, 128:] = (rest + pltpu.roll(rest, 64, 1))[:, :64]
            return 0

        for s in range(PARTS):
            pcol_wait(3, s, cut, s4, r4)
        lax.fori_loop(0, YB // 4, step, 0)

    loads[CUTS].wait()
    forward_z(0)
    for load in loads[CUTS + 1 :]:
        load.wait()
    forward_z(1)
    for s in range(PARTS):
        block = jnp.concatenate([ker[s * K4 + m // 2] for m in range(8)], axis=0)
        weight[s] = jnp.concatenate([block, jnp.zeros((W, 64), F32)], axis=1).T[:N]
    forward_y((0, 1, 2), 0)
    forward_z(2)
    forward_y((0, 1, 2), 1)
    forward_y((0,), 2)
    forward_y((1,), 2)
    middle_x(0)
    forward_y((2,), 2)
    middle_x(1)
    backward_y(0, (0, 1, 2))
    middle_x(2)
    backward_y(1, (0, 1, 2))
    for cut in range(CUTS):
        backward_y(2, (cut,))
    for cut in range(CUTS):
        backward_z(cut)

    for cut in range(CUTS):
        band_copy(cut).wait_send()
        for s in range(PARTS):
            pcol_sent(0, s, cut, s1)
            prow_sent(1, s, cut, s2)
            prow_sent(2, s, cut, s3)
            pcol_sent(3, s, cut, s4)


def on_device(orbitals, kernel, plan, occupation):
    orb = jnp.transpose(orbitals, (0, 2, 1, 3))
    ker = jnp.transpose(kernel, (1, 0, 2))
    tables = jnp.asarray(np.stack(make_tables()))
    pcol_buf = pltpu.VMEM((PARTS, CUTS, PC * CH, 128), F32)
    prow_buf = pltpu.VMEM((PARTS, PR, CUTS, 2 * XC, W), F32)
    vmem = pl.BlockSpec(memory_space=pltpu.VMEM)
    out = pl.pallas_call(
        body,
        out_shape=jax.ShapeDtypeStruct((2, YB * XB, N), F32),
        in_specs=[pl.BlockSpec(memory_space=pltpu.SMEM)] * 2 + [pl.BlockSpec(memory_space=pl.ANY)] * 3,
        out_specs=vmem,
        scratch_shapes=[
            pltpu.VMEM((CUTS, 2, YB, XC, N), F32),
            pltpu.VMEM((YB, XB, N), F32),
            pltpu.VMEM((PARTS, N, W), F32),
            pltpu.VMEM((12, W, W), BF16),
            pltpu.VMEM((YB * XB, W), F32),
            pltpu.VMEM((YB * XB, W), F32),
            pltpu.VMEM((YB * XB, W), F32),
            pcol_buf, pcol_buf, prow_buf, prow_buf, prow_buf, prow_buf, pcol_buf, pcol_buf,
            pltpu.SemaphoreType.DMA((10,)),
            pltpu.SemaphoreType.DMA((3,)),
            pltpu.SemaphoreType.DMA((3,)),
            pltpu.SemaphoreType.DMA((4, PARTS, CUTS)),
            pltpu.SemaphoreType.DMA((4, PARTS, CUTS)),
            pltpu.SemaphoreType.DMA((4, PARTS, CUTS)),
        ],
        compiler_params=pltpu.CompilerParams(
            collective_id=0, has_side_effects=True, vmem_limit_bytes=56 * 2**20
        ),
    )(plan, occupation, orb, ker, tables)
    return jnp.transpose(out.reshape(2, YB, XB, N), (0, 2, 1, 3))


def solution(mesh):
    return jax.shard_map(
        on_device,
        mesh=mesh,
        in_specs=(P("band", "prow", "pcol", None), P("prow", "pcol", None), P(), P()),
        out_specs=P("band", "prow", "pcol", None),
        check_vma=False,
    )
```

time: 106 us -> 89.8 us (0.85)
  Pallas kernels: 104 us -> 87.3 us
    pallas_call x1, Pallas kernels: 104 us -> 87.3 us  [on_device(): pl.pallas_call(body, out_shape=jax.ShapeDtypeStruct((2, YB * XB, N), F32)...]
where the time goes in v3:
time: 89.8 us; the launch traced here: 89.7 us
  Pallas kernels  87.3 us (97%)
  local copies, waits for them, and re-layouts  2.37 us (3%)
    pallas_call x1, Pallas kernels, on_device(): pl.pallas_call(body, out_shape=jax.ShapeDtypeStruct((2, YB * XB, N), F32)...  87.3 us
    unnamed x1, local copies, waits for them, and re-layouts  2.37 us

profile of v3, /device:TPU:1, one launch (start us, length us, event | category | flops | bytes accessed | tf_op | source)
XLA Modules:
  0.0 89.7 jit_solution(8307683788131271924)
XLA Ops:
  0.0 87.3 %shard_map.55 = f32[2,576,192]{2,1,0:T(8,128)} custom-call(s32[4]{0:T(128)} %plan_ref.1, s32[4]{0:T(128)} %occ_ref.1, f32[2,12,48,192]{3,2,1,0:T(8,128)} %bitcast.6, f32[12,48,192]{2,1,0:T(8,128)} %bitcast.7, bf16[12,384,384]{2,1,0:T(8,128)(2,1)} %constant.2.clone.tables_hbm), custom_call_target="tpu_custom_call" | custom-call | tf_op jit(solution)/shard_map/pallas_call | solution.py:398
  87.3 2.4 %copy.7 = f32[2,48,12,192]{3,1,2,0:T(8,128)} copy(f32[2,48,12,192]{3,1,2,0:T(8,128)} %bitcast.5) | data formatting | bytes 1769472

commit v4 on v3

--- a/solution.py
+++ b/solution.py
@@ -69,10 +69,10 @@
 
 
 def dot3(left, right, dims):
-    def dot(a, b):
-        return lax.dot_general(a, b, (dims, ((), ())), preferred_element_type=F32)
-
-    return dot(left[0], right[0]) + (dot(left[0], right[1]) + dot(left[1], right[0]))
+    (left_dim,), (right_dim,) = dims
+    long_left = jnp.concatenate([left[0], left[0], left[1]], axis=left_dim)
+    long_right = jnp.concatenate([right[0], right[1], right[0]], axis=right_dim)
+    return lax.dot_general(long_left, long_right, (dims, ((), ())), preferred_element_type=F32)
 
 
 NN = ((1,), (0,))
@@ -115,10 +115,9 @@
     barrier = pltpu.get_barrier_semaphore()
 
     def greet_p(k, _):
-        to = lax.rem(me_p * 2 + me_b + k, 2 * PC)
-        pl.semaphore_signal(
-            barrier, inc=1, device_id={"pcol": to // 2, "band": lax.rem(to, 2)}, device_id_type=MESH
-        )
+        to = lax.rem(me_p + k, PC)
+        band = lax.rem(work + lax.rem(to // 2, 2), 2)
+        pl.semaphore_signal(barrier, inc=1, device_id={"pcol": to, "band": band}, device_id_type=MESH)
         return 0
 
     def greet_r(k, _):
@@ -138,8 +137,11 @@
     loads.append(pltpu.make_async_copy(ker_hbm, ker, load_sem.at[3]))
     for load in loads[: CUTS + 1]:
         load.start()
-    lax.fori_loop(1, 2 * PC, greet_p, 0)
-    lax.fori_loop(1, PR, greet_r, 0)
+    pl.semaphore_signal(barrier, inc=1, device_id={"band": partner}, device_id_type=MESH)
+    for k in range(1, PC):
+        greet_p(k, 0)
+    for k in range(1, PR):
+        greet_r(k, 0)
 
     rows = YB * XC
 
@@ -161,7 +163,7 @@
             mine[at, 128:256] = orb[cut, 1, y, :, :128]
             mine[at, 256:] = jnp.concatenate([orb[cut, 0, y, :, 128:], orb[cut, 1, y, :, 128:]], axis=1)
         if cut == 0:
-            pl.semaphore_wait(barrier, 2 * PC - 1 + PR - 1)
+            pl.semaphore_wait(barrier, 1 + PC - 1 + PR - 1)
         band_copy(cut).start()
     for load in loads[CUTS + 1 :]:
         load.start()
@@ -289,7 +291,9 @@
 
         band_copy(cut).wait_recv()
         lax.fori_loop(0, YB // 4, step, 0)
-        for s in range(PARTS):
+
+    def send_z(*which):
+        for s, cut in which:
             pcol_start(0, s, cut, s1, r1)
 
     def forward_y(parts, cut):
@@ -357,22 +361,25 @@
 
     loads[CUTS].wait()
     forward_z(0)
+    send_z((0, 0), (1, 0), (2, 0))
     for load in loads[CUTS + 1 :]:
         load.wait()
     forward_z(1)
+    send_z((0, 1), (1, 1), (2, 1))
     for s in range(PARTS):
         block = jnp.concatenate([ker[s * K4 + m // 2] for m in range(8)], axis=0)
         weight[s] = jnp.concatenate([block, jnp.zeros((W, 64), F32)], axis=1).T[:N]
     forward_y((0, 1, 2), 0)
     forward_z(2)
+    send_z((0, 2), (1, 2), (2, 2))
     forward_y((0, 1, 2), 1)
     forward_y((0,), 2)
     forward_y((1,), 2)
+    forward_y((2,), 2)
     middle_x(0)
-    forward_y((2,), 2)
     middle_x(1)
+    middle_x(2)
     backward_y(0, (0, 1, 2))
-    middle_x(2)
     backward_y(1, (0, 1, 2))
     for cut in range(CUTS):
         backward_y(2, (cut,))

time: 89.8 us -> 87.8 us (0.978)
  Pallas kernels: 87.3 us -> 85.3 us
    pallas_call x1, Pallas kernels: 87.3 us -> 85.3 us  [on_device(): pl.pallas_call(body, out_shape=jax.ShapeDtypeStruct((2, YB * XB, N), F32)...]
where the time goes in v4:
time: 87.8 us; the launch traced here: 87.6 us
  Pallas kernels  85.3 us (97%)
  local copies, waits for them, and re-layouts  2.37 us (3%)
    pallas_call x1, Pallas kernels, on_device(): pl.pallas_call(body, out_shape=jax.ShapeDtypeStruct((2, YB * XB, N), F32)...  85.3 us
    unnamed x1, local copies, waits for them, and re-layouts  2.37 us

profile of v4, /device:TPU:1, one launch (start us, length us, event | category | flops | bytes accessed | tf_op | source)
XLA Modules:
  0.0 87.6 jit_solution(7555638529061677126)
XLA Ops:
  0.0 85.3 %shard_map.55 = f32[2,576,192]{2,1,0:T(8,128)} custom-call(s32[4]{0:T(128)} %plan_ref.1, s32[4]{0:T(128)} %occ_ref.1, f32[2,12,48,192]{3,2,1,0:T(8,128)} %bitcast.6, f32[12,48,192]{2,1,0:T(8,128)} %bitcast.7, bf16[12,384,384]{2,1,0:T(8,128)(2,1)} %constant.2.clone.tables_hbm), custom_call_target="tpu_custom_call" | custom-call | tf_op jit(solution)/shard_map/pallas_call | solution.py:405
  85.3 2.4 %copy.7 = f32[2,48,12,192]{3,1,2,0:T(8,128)} copy(f32[2,48,12,192]{3,1,2,0:T(8,128)} %bitcast.5) | data formatting | bytes 1769472

commit v5 on v4

--- a/solution.py
+++ b/solution.py
@@ -18,6 +18,7 @@
 K4 = 4
 CUTS = 3
 XC = 16
+BAND_PIECES = (3, 3, 3)
 W = 384
 CH = 24
 F32 = jnp.float32
@@ -100,7 +101,7 @@
     plan_ref, occ_ref, orb_hbm, ker_hbm, tables_hbm,
     out_ref,
     orb, ker, weight, tables, mine, other, psi, s1, r1, s2, r2, s3, r3, s4, r4,
-    load_sem, psi_send, psi_recv, own_sem, send_sem, recv_sem,
+    load_sem, pcol_sems, psi_send, psi_recv, own_sem, send_sem, recv_sem,
 ):
     def table(t):
         return tables[2 * t], tables[2 * t + 1]
@@ -145,12 +146,14 @@
 
     rows = YB * XC
 
-    def band_copy(cut):
+    def band_copy(cut, piece):
+        size = rows // BAND_PIECES[cut]
+        at = pl.ds(cut * rows + piece * size, size)
         return pltpu.make_async_remote_copy(
-            src_ref=mine.at[pl.ds(cut * rows, rows)],
-            dst_ref=other.at[pl.ds(cut * rows, rows)],
-            send_sem=psi_send.at[cut],
-            recv_sem=psi_recv.at[cut],
+            src_ref=mine.at[at],
+            dst_ref=other.at[at],
+            send_sem=psi_send.at[cut, piece],
+            recv_sem=psi_recv.at[cut, piece],
             device_id={"band": partner},
             device_id_type=MESH,
         )
@@ -162,9 +165,10 @@
             mine[at, :128] = orb[cut, 0, y, :, :128]
             mine[at, 128:256] = orb[cut, 1, y, :, :128]
             mine[at, 256:] = jnp.concatenate([orb[cut, 0, y, :, 128:], orb[cut, 1, y, :, 128:]], axis=1)
-        if cut == 0:
-            pl.semaphore_wait(barrier, 1 + PC - 1 + PR - 1)
-        band_copy(cut).start()
+            if cut == 0 and y == YB // BAND_PIECES[0] - 1:
+                pl.semaphore_wait(barrier, 1 + PC - 1 + PR - 1)
+            if (y + 1) % (YB // BAND_PIECES[cut]) == 0:
+                band_copy(cut, (y + 1) // (YB // BAND_PIECES[cut]) - 1).start()
     for load in loads[CUTS + 1 :]:
         load.start()
 
@@ -202,34 +206,46 @@
             jnp.concatenate([low * source[0], low * source[1], up * source[2]], axis=1) for low, up in phi
         ]
 
-    def pcol_start(e, s, cut, src, dst):
-        here = pl.ds(me_p * CH, CH)
+    numbers = {}
+
+    def pcol_at(ref, bundle, owner, count=1):
+        s, parts, cut, cuts, y, ys = bundle
+        first, size = (owner * CH + 2 * y, 2 * ys) if count == 1 else (0, 2 * ys * count)
+        return ref.at[pl.ds(s, parts), pl.ds(cut, cuts), pl.ds(first, size), :]
+
+    def pcol_own(e, bundle, src, dst):
+        sem = pcol_sems.at[2, numbers[e, bundle]]
+        return pltpu.make_async_copy(pcol_at(src, bundle, me_p), pcol_at(dst, bundle, me_p), sem)
+
+    def pcol_start(e, bundle, src, dst):
+        number = numbers.setdefault((e, bundle), len(numbers))
 
         def send(k, _):
             to = lax.rem(me_p + k, PC)
             band = lax.rem(work + lax.rem(to // 2, 2), 2) if e == 0 else work
             pltpu.make_async_remote_copy(
-                src_ref=src.at[s, cut, pl.ds(to * CH, CH), :],
-                dst_ref=dst.at[s, cut, here, :],
-                send_sem=send_sem.at[e, s, cut],
-                recv_sem=recv_sem.at[e, s, cut],
+                src_ref=pcol_at(src, bundle, to),
+                dst_ref=pcol_at(dst, bundle, me_p),
+                send_sem=pcol_sems.at[0, number],
+                recv_sem=pcol_sems.at[1, number],
                 device_id={"pcol": to, "band": band},
                 device_id_type=MESH,
             ).start()
             return 0
 
-        own = pltpu.make_async_copy(src.at[s, cut, here, :], dst.at[s, cut, here, :], own_sem.at[e, s, cut])
+        own = pcol_own(e, bundle, src, dst)
         if e == 0:
-            lax.fori_loop(1, PC, send, 0)
+            for k in range(1, PC):
+                send(k, 0)
             own.start()
         else:
             lax.fori_loop(1 - half, PC, send, 0)
             pl.when(half == 0)(own.start)
 
-    def pcol_all(sem, e, s, cut, ref):
+    def pcol_all(which, e, bundle, ref):
         def wait_for(count):
-            part = ref.at[s, cut, pl.ds(0, count * CH), :]
-            return pltpu.make_async_copy(part, part, sem.at[e, s, cut]).wait
+            part = pcol_at(ref, bundle, 0, count)
+            return pltpu.make_async_copy(part, part, pcol_sems.at[which, numbers[e, bundle]]).wait
 
         if e == 0:
             wait_for(PC - 1)()
@@ -237,17 +253,31 @@
             pl.when(half == 0)(wait_for(PC - 1))
             pl.when(half == 1)(wait_for(PC))
 
-    def pcol_wait(e, s, cut, src, dst):
-        here = pl.ds(me_p * CH, CH)
-        own = pltpu.make_async_copy(src.at[s, cut, here, :], dst.at[s, cut, here, :], own_sem.at[e, s, cut])
+    waited = set()
+
+    def pcol_wait(e, bundle, src, dst):
+        if (e, bundle) in waited:
+            return
+        waited.add((e, bundle))
+        own = pcol_own(e, bundle, src, dst)
         if e == 0:
             own.wait()
         else:
             pl.when(half == 0)(own.wait)
-        pcol_all(recv_sem, e, s, cut, dst)
-
-    def pcol_sent(e, s, cut, src):
-        pcol_all(send_sem, e, s, cut, src)
+        pcol_all(1, e, bundle, dst)
+
+    def pcol_sent(e, bundle, src):
+        pcol_all(0, e, bundle, src)
+
+    Y_PIECES = (3, 3, 3)
+
+    def forward_bundles(s, cut):
+        if cut < len(Y_PIECES):
+            return [(0, PARTS, cut, 1, y, YB // Y_PIECES[cut]) for y in range(0, YB, YB // Y_PIECES[cut])]
+        return [(s, 1, cut, 1, 0, YB)]
+
+    def back_bundle(s, cut):
+        return (s, 1, 0, CUTS, 0, YB) if s < 0 else (s, 1, cut, 1, 0, YB)
 
     def prow_start(e, s, cut, src, dst):
         def send(k, _):
@@ -289,16 +319,20 @@
                         s1[s, cut, pl.ds((group * 4 + y4) * 2 + c, PC, stride=CH), :] = spec[y4][first : first + PC]
             return 0
 
-        band_copy(cut).wait_recv()
-        lax.fori_loop(0, YB // 4, step, 0)
-
-    def send_z(*which):
-        for s, cut in which:
-            pcol_start(0, s, cut, s1, r1)
+        for piece in range(BAND_PIECES[cut]):
+            band_copy(cut, piece).wait_recv()
+            groups = YB // 4 // BAND_PIECES[cut]
+            lax.fori_loop(piece * groups, (piece + 1) * groups, step, 0)
+            for s in range(PARTS):
+                for bundle in forward_bundles(s, cut):
+                    ready = (piece + 1) * groups * 4
+                    if bundle[4] + bundle[5] <= ready and (0, bundle) not in numbers:
+                        pcol_start(0, bundle, s1, r1)
 
     def forward_y(parts, cut):
         for s in parts:
-            pcol_wait(0, s, cut, s1, r1)
+            for bundle in forward_bundles(s, cut):
+                pcol_wait(0, bundle, s1, r1)
         turned = jnp.concatenate([r1[s, cut].T for s in parts], axis=0)
         spec = dot3(halves(turned), table(1), NN)
         for i, s in enumerate(parts):
@@ -326,7 +360,8 @@
         back = dot3(table(4), halves(jnp.concatenate(data, axis=0)), NT)
         for i, cut in enumerate(cuts):
             s4[s, cut] = back[:, i * 128 : (i + 1) * 128]
-            pcol_start(3, s, cut, s4, r4)
+            if cut == CUTS - 1 or back_bundle(s, cut) != back_bundle(s, cut + 1):
+                pcol_start(3, back_bundle(s, cut), s4, r4)
 
     def backward_z(cut):
         def step(group, _):
@@ -356,22 +391,19 @@
             return 0
 
         for s in range(PARTS):
-            pcol_wait(3, s, cut, s4, r4)
+            pcol_wait(3, back_bundle(s, cut), s4, r4)
         lax.fori_loop(0, YB // 4, step, 0)
 
     loads[CUTS].wait()
     forward_z(0)
-    send_z((0, 0), (1, 0), (2, 0))
     for load in loads[CUTS + 1 :]:
         load.wait()
     forward_z(1)
-    send_z((0, 1), (1, 1), (2, 1))
     for s in range(PARTS):
         block = jnp.concatenate([ker[s * K4 + m // 2] for m in range(8)], axis=0)
         weight[s] = jnp.concatenate([block, jnp.zeros((W, 64), F32)], axis=1).T[:N]
     forward_y((0, 1, 2), 0)
     forward_z(2)
-    send_z((0, 2), (1, 2), (2, 2))
     forward_y((0, 1, 2), 1)
     forward_y((0,), 2)
     forward_y((1,), 2)
@@ -379,20 +411,22 @@
     middle_x(0)
     middle_x(1)
     middle_x(2)
-    backward_y(0, (0, 1, 2))
-    backward_y(1, (0, 1, 2))
+    for part in (0, 1):
+        for cut in range(CUTS):
+            backward_y(part, (cut,))
     for cut in range(CUTS):
         backward_y(2, (cut,))
     for cut in range(CUTS):
         backward_z(cut)
 
     for cut in range(CUTS):
-        band_copy(cut).wait_send()
+        for piece in range(BAND_PIECES[cut]):
+            band_copy(cut, piece).wait_send()
         for s in range(PARTS):
-            pcol_sent(0, s, cut, s1)
             prow_sent(1, s, cut, s2)
             prow_sent(2, s, cut, s3)
-            pcol_sent(3, s, cut, s4)
+    for e, bundle in numbers:
+        pcol_sent(e, bundle, s1 if e == 0 else s4)
 
 
 def on_device(orbitals, kernel, plan, occupation):
@@ -417,8 +451,9 @@
             pltpu.VMEM((YB * XB, W), F32),
             pcol_buf, pcol_buf, prow_buf, prow_buf, prow_buf, prow_buf, pcol_buf, pcol_buf,
             pltpu.SemaphoreType.DMA((10,)),
-            pltpu.SemaphoreType.DMA((3,)),
-            pltpu.SemaphoreType.DMA((3,)),
+            pltpu.SemaphoreType.DMA((3, 24)),
+            pltpu.SemaphoreType.DMA((CUTS, 3)),
+            pltpu.SemaphoreType.DMA((CUTS, 3)),
             pltpu.SemaphoreType.DMA((4, PARTS, CUTS)),
             pltpu.SemaphoreType.DMA((4, PARTS, CUTS)),
             pltpu.SemaphoreType.DMA((4, PARTS, CUTS)),

time: 87.8 us -> 79.2 us (0.902)
  Pallas kernels: 85.3 us -> 76.6 us
    pallas_call x1, Pallas kernels: 85.3 us -> 76.6 us  [on_device(): pl.pallas_call(body, out_shape=jax.ShapeDtypeStruct((2, YB * XB, N), F32)...]
where the time goes in v5:
time: 79.2 us; the launch traced here: 79 us
  Pallas kernels  76.6 us (97%)
  local copies, waits for them, and re-layouts  2.37 us (3%)
    pallas_call x1, Pallas kernels, on_device(): pl.pallas_call(body, out_shape=jax.ShapeDtypeStruct((2, YB * XB, N), F32)...  76.6 us
    unnamed x1, local copies, waits for them, and re-layouts  2.37 us

profile of v5, /device:TPU:1, one launch (start us, length us, event | category | flops | bytes accessed | tf_op | source)
XLA Modules:
  0.0 79.0 jit_solution(17722358579151152207)
XLA Ops:
  0.0 76.6 %shard_map.55 = f32[2,576,192]{2,1,0:T(8,128)} custom-call(s32[4]{0:T(128)} %plan_ref.1, s32[4]{0:T(128)} %occ_ref.1, f32[2,12,48,192]{3,2,1,0:T(8,128)} %bitcast.6, f32[12,48,192]{2,1,0:T(8,128)} %bitcast.7, bf16[12,384,384]{2,1,0:T(8,128)(2,1)} %constant.2.clone.tables_hbm), custom_call_target="tpu_custom_call" | custom-call | tf_op jit(solution)/shard_map/pallas_call | solution.py:439
  76.7 2.4 %copy.7 = f32[2,48,12,192]{3,1,2,0:T(8,128)} copy(f32[2,48,12,192]{3,1,2,0:T(8,128)} %bitcast.5) | data formatting | bytes 1769472

commit v6 on v5

--- a/solution.py
+++ b/solution.py
@@ -136,14 +136,15 @@
         for t in range(6)
     ]
     loads.append(pltpu.make_async_copy(ker_hbm, ker, load_sem.at[3]))
-    for load in loads[: CUTS + 1]:
-        load.start()
+    loads[0].start()
     pl.semaphore_signal(barrier, inc=1, device_id={"band": partner}, device_id_type=MESH)
     for k in range(1, PC):
         greet_p(k, 0)
     for k in range(1, PR):
         greet_r(k, 0)
 
+    for load in loads[1 : CUTS + 1]:
+        load.start()
     rows = YB * XC
 
     def band_copy(cut, piece):
@@ -276,8 +277,10 @@
             return [(0, PARTS, cut, 1, y, YB // Y_PIECES[cut]) for y in range(0, YB, YB // Y_PIECES[cut])]
         return [(s, 1, cut, 1, 0, YB)]
 
-    def back_bundle(s, cut):
-        return (s, 1, 0, CUTS, 0, YB) if s < 0 else (s, 1, cut, 1, 0, YB)
+    def back_bundles(s, cut):
+        if s == PARTS - 1:
+            return [(s, 1, cut, 1, y, 4) for y in range(0, YB, 4)]
+        return [(s, 1, cut, 1, 0, YB)]
 
     def prow_start(e, s, cut, src, dst):
         def send(k, _):
@@ -292,7 +295,8 @@
             ).start()
             return 0
 
-        lax.fori_loop(1, PR, send, 0)
+        for k in range(1, PR):
+            send(k, 0)
         pltpu.make_async_copy(src.at[s, me_r, cut], dst.at[s, me_r, cut], own_sem.at[e, s, cut]).start()
 
     def prow_wait(e, s, cut, src, dst):
@@ -360,8 +364,8 @@
         back = dot3(table(4), halves(jnp.concatenate(data, axis=0)), NT)
         for i, cut in enumerate(cuts):
             s4[s, cut] = back[:, i * 128 : (i + 1) * 128]
-            if cut == CUTS - 1 or back_bundle(s, cut) != back_bundle(s, cut + 1):
-                pcol_start(3, back_bundle(s, cut), s4, r4)
+            for bundle in back_bundles(s, cut):
+                pcol_start(3, bundle, s4, r4)
 
     def backward_z(cut):
         def step(group, _):
@@ -390,18 +394,19 @@
                     out_ref[j, at, 128:] = (rest + pltpu.roll(rest, 64, 1))[:, :64]
             return 0
 
-        for s in range(PARTS):
-            pcol_wait(3, back_bundle(s, cut), s4, r4)
-        lax.fori_loop(0, YB // 4, step, 0)
-
-    loads[CUTS].wait()
-    forward_z(0)
-    for load in loads[CUTS + 1 :]:
+        for group in range(YB // 4):
+            for s in range(PARTS):
+                bundles = back_bundles(s, cut)
+                pcol_wait(3, bundles[group % len(bundles)], s4, r4)
+            step(group, 0)
+
+    for load in loads[CUTS:]:
         load.wait()
-    forward_z(1)
     for s in range(PARTS):
         block = jnp.concatenate([ker[s * K4 + m // 2] for m in range(8)], axis=0)
         weight[s] = jnp.concatenate([block, jnp.zeros((W, 64), F32)], axis=1).T[:N]
+    forward_z(0)
+    forward_z(1)
     forward_y((0, 1, 2), 0)
     forward_z(2)
     forward_y((0, 1, 2), 1)
@@ -451,7 +456,7 @@
             pltpu.VMEM((YB * XB, W), F32),
             pcol_buf, pcol_buf, prow_buf, prow_buf, prow_buf, prow_buf, pcol_buf, pcol_buf,
             pltpu.SemaphoreType.DMA((10,)),
-            pltpu.SemaphoreType.DMA((3, 24)),
+            pltpu.SemaphoreType.DMA((3, 32)),
             pltpu.SemaphoreType.DMA((CUTS, 3)),
             pltpu.SemaphoreType.DMA((CUTS, 3)),
             pltpu.SemaphoreType.DMA((4, PARTS, CUTS)),

time: 79.2 us -> 79.1 us (level)
  no operation moved by 1% of the time
where the time goes in v6:
time: 79.1 us; the launch traced here: 78.9 us
  Pallas kernels  76.5 us (97%)
  local copies, waits for them, and re-layouts  2.37 us (3%)
    pallas_call x1, Pallas kernels, on_device(): pl.pallas_call(body, out_shape=jax.ShapeDtypeStruct((2, YB * XB, N), F32)...  76.5 us
    unnamed x1, local copies, waits for them, and re-layouts  2.37 us

profile of v6, /device:TPU:1, one launch (start us, length us, event | category | flops | bytes accessed | tf_op | source)
XLA Modules:
  0.0 78.9 jit_solution(11814423180111679614)
XLA Ops:
  0.0 76.5 %shard_map.55 = f32[2,576,192]{2,1,0:T(8,128)} custom-call(s32[4]{0:T(128)} %plan_ref.1, s32[4]{0:T(128)} %occ_ref.1, f32[2,12,48,192]{3,2,1,0:T(8,128)} %bitcast.6, f32[12,48,192]{2,1,0:T(8,128)} %bitcast.7, bf16[12,384,384]{2,1,0:T(8,128)(2,1)} %constant.2.clone.tables_hbm), custom_call_target="tpu_custom_call" | custom-call | tf_op jit(solution)/shard_map/pallas_call | solution.py:444
  76.5 2.4 %copy.7 = f32[2,48,12,192]{3,1,2,0:T(8,128)} copy(f32[2,48,12,192]{3,1,2,0:T(8,128)} %bitcast.5) | data formatting | bytes 1769472

commit v7 on v5

--- a/solution.py
+++ b/solution.py
@@ -100,8 +100,8 @@
 def body(
     plan_ref, occ_ref, orb_hbm, ker_hbm, tables_hbm,
     out_ref,
-    orb, ker, weight, tables, mine, other, psi, s1, r1, s2, r2, s3, r3, s4, r4,
-    load_sem, pcol_sems, psi_send, psi_recv, own_sem, send_sem, recv_sem,
+    orb, result, ker, weight, tables, mine, other, psi, s1, r1, s2, r2, s3, r3, s4, r4,
+    load_sem, put_sem, pcol_sems, psi_send, psi_recv, own_sem, send_sem, recv_sem,
 ):
     def table(t):
         return tables[2 * t], tables[2 * t + 1]
@@ -292,7 +292,8 @@
             ).start()
             return 0
 
-        lax.fori_loop(1, PR, send, 0)
+        for k in range(1, PR):
+            send(k, 0)
         pltpu.make_async_copy(src.at[s, me_r, cut], dst.at[s, me_r, cut], own_sem.at[e, s, cut]).start()
 
     def prow_wait(e, s, cut, src, dst):
@@ -362,6 +363,9 @@
             s4[s, cut] = back[:, i * 128 : (i + 1) * 128]
             if cut == CUTS - 1 or back_bundle(s, cut) != back_bundle(s, cut + 1):
                 pcol_start(3, back_bundle(s, cut), s4, r4)
+
+    def put(cut):
+        return pltpu.make_async_copy(result.at[cut], out_ref.at[:, :, pl.ds(cut * XC, XC), :], put_sem.at[cut])
 
     def backward_z(cut):
         def step(group, _):
@@ -381,18 +385,18 @@
             for y4 in range(4):
                 y = group * 4 + y4
                 source = psi[pl.ds(pl.multiple_of(cut * rows + y * XC, 16), XC), :]
-                at = pl.ds(pl.multiple_of(y * XB + cut * XC, 16), XC)
                 for j in range(2):
                     first = (y4 * 2 + j) * XC
                     term = field[first : first + XC] * source
                     rest = term[:, 256:]
-                    out_ref[j, at, :128] = term[:, :128] + term[:, 128:256]
-                    out_ref[j, at, 128:] = (rest + pltpu.roll(rest, 64, 1))[:, :64]
+                    result[cut, j, y, :, :128] = term[:, :128] + term[:, 128:256]
+                    result[cut, j, y, :, 128:] = (rest + pltpu.roll(rest, 64, 1))[:, :64]
             return 0
 
         for s in range(PARTS):
             pcol_wait(3, back_bundle(s, cut), s4, r4)
         lax.fori_loop(0, YB // 4, step, 0)
+        put(cut).start()
 
     loads[CUTS].wait()
     forward_z(0)
@@ -420,6 +424,7 @@
         backward_z(cut)
 
     for cut in range(CUTS):
+        put(cut).wait()
         for piece in range(BAND_PIECES[cut]):
             band_copy(cut, piece).wait_send()
         for s in range(PARTS):
@@ -435,13 +440,13 @@
     tables = jnp.asarray(np.stack(make_tables()))
     pcol_buf = pltpu.VMEM((PARTS, CUTS, PC * CH, 128), F32)
     prow_buf = pltpu.VMEM((PARTS, PR, CUTS, 2 * XC, W), F32)
-    vmem = pl.BlockSpec(memory_space=pltpu.VMEM)
     out = pl.pallas_call(
         body,
-        out_shape=jax.ShapeDtypeStruct((2, YB * XB, N), F32),
+        out_shape=jax.ShapeDtypeStruct((2, YB, XB, N), F32),
         in_specs=[pl.BlockSpec(memory_space=pltpu.SMEM)] * 2 + [pl.BlockSpec(memory_space=pl.ANY)] * 3,
-        out_specs=vmem,
+        out_specs=pl.BlockSpec(memory_space=pl.ANY),
         scratch_shapes=[
+            pltpu.VMEM((CUTS, 2, YB, XC, N), F32),
             pltpu.VMEM((CUTS, 2, YB, XC, N), F32),
             pltpu.VMEM((YB, XB, N), F32),
             pltpu.VMEM((PARTS, N, W), F32),
@@ -451,6 +456,7 @@
             pltpu.VMEM((YB * XB, W), F32),
             pcol_buf, pcol_buf, prow_buf, prow_buf, prow_buf, prow_buf, pcol_buf, pcol_buf,
             pltpu.SemaphoreType.DMA((10,)),
+            pltpu.SemaphoreType.DMA((CUTS,)),
             pltpu.SemaphoreType.DMA((3, 24)),
             pltpu.SemaphoreType.DMA((CUTS, 3)),
             pltpu.SemaphoreType.DMA((CUTS, 3)),
@@ -462,7 +468,7 @@
             collective_id=0, has_side_effects=True, vmem_limit_bytes=56 * 2**20
         ),
     )(plan, occupation, orb, ker, tables)
-    return jnp.transpose(out.reshape(2, YB, XB, N), (0, 2, 1, 3))
+    return jnp.transpose(out, (0, 2, 1, 3))
 
 
 def solution(mesh):

time: 79.2 us -> 79 us (level)
  no operation moved by 1% of the time
where the time goes in v7:
time: 79 us; the launch traced here: 78.8 us
  Pallas kernels  76.4 us (97%)
  local copies, waits for them, and re-layouts  2.37 us (3%)
    pallas_call x1, Pallas kernels, on_device(): pl.pallas_call(body, out_shape=jax.ShapeDtypeStruct((2, YB, XB, N), F32),...  76.4 us
    unnamed x1, local copies, waits for them, and re-layouts  2.37 us

profile of v7, /device:TPU:1, one launch (start us, length us, event | category | flops | bytes accessed | tf_op | source)
XLA Modules:
  0.0 78.8 jit_solution(965217831961164443)
XLA Ops:
  0.0 76.4 %shard_map.55 = f32[2,12,48,192]{3,2,1,0:T(8,128)} custom-call(s32[4]{0:T(128)} %plan_ref.1, s32[4]{0:T(128)} %occ_ref.1, f32[2,12,48,192]{3,2,1,0:T(8,128)} %bitcast.4, f32[12,48,192]{2,1,0:T(8,128)} %bitcast.5, bf16[12,384,384]{2,1,0:T(8,128)(2,1)} %constant.2.clone.tables_hbm), custom_call_target="tpu_custom_call" | custom-call | tf_op jit(solution)/shard_map/pallas_call | solution.py:443
  76.4 2.4 %copy.7 = f32[2,48,12,192]{3,1,2,0:T(8,128)} copy(f32[2,48,12,192]{3,1,2,0:T(8,128)} %bitcast.3) | data formatting | bytes 1769472
